TPU v7x, 32 devices: a whole 2x2x4 slice. The times are simulated.
32 devices in a mesh: dp: 2 (over core), head: 4 (over y, x), ctx: 4 (over z).
Axes of the slice: x: 2, y: 2, z: 4, core: 2. Of those that a mesh axis runs over, the one named last changes fastest.
Arguments:
- q_raw: bfloat16 [2, 512, 4096], P('dp', 'ctx', 'head'), may hold values from -6 to 6
- k_raw: bfloat16 [2, 512, 4096], P('dp', 'ctx', 'head'), may hold values from -6 to 6
- v_raw: bfloat16 [2, 512, 4096], P('dp', 'ctx', 'head'), may hold values from -6 to 6
- conv_weight: float32 [3, 4, 4096], P(None, None, 'head'), may hold values from -4 to 4
- decay_logit: float32 [2, 512, 32], P('dp', 'ctx', 'head'), may hold values from -8 to 8
- beta_logit: float32 [2, 512, 32], P('dp', 'ctx', 'head'), may hold values from -8 to 8
- decay_rate: float32 [32], P('head'), may hold values from 0.00048828125 to 0.05
- block_resets: int32 [2, 4], P('dp', 'ctx'), may hold values from 0 to 1
- norm_gain: float32 [4096], P('head'), may hold values from 0.25 to 1.75
- d_out: bfloat16 [2, 512, 4096], P('dp', 'ctx', 'head'), may hold values from -6 to 6
Outputs:
- out: bfloat16 [2, 512, 4096], P('dp', 'ctx', 'head')
- d_q_raw: bfloat16 [2, 512, 4096], P('dp', 'ctx', 'head')
- d_k_raw: bfloat16 [2, 512, 4096], P('dp', 'ctx', 'head')
- d_v_raw: bfloat16 [2, 512, 4096], P('dp', 'ctx', 'head')
- d_conv_weight: float32 [3, 4, 4096], P(None, None, 'head')
- d_decay_logit: float32 [2, 512, 32], P('dp', 'ctx', 'head')
- d_beta_logit: float32 [2, 512, 32], P('dp', 'ctx', 'head')
- d_decay_rate: float32 [32], P('head')
- d_norm_gain: float32 [4096], P('head')
All inputs are finite; a program needn't handle non-finite values.
Results may differ from a plain program's by a relative error of at most 0.0019.
Values may be sent and summed in bfloat16 or wider, within the bound.
A program may use at most 128 MiB of HBM per device.

v0:
```python
import jax
import jax.numpy as jnp
from jax import lax
from jax.sharding import PartitionSpec as P

BLOCK_LENGTH = 128


highest = lax.Precision.HIGHEST


def shifted(value, axis, steps):
    count = lax.axis_size(axis)
    leading, last = (max(0, -steps), min(count, count - steps))
    return lax.ppermute(value, axis, [(source, source + steps) for source in range(leading, last)])


def entering(part, axis, combine, identity):
    count = lax.axis_size(axis)
    place = lax.axis_index(axis)
    ahead = count - 1 - place
    gathered = jax.tree.map(lambda a: lax.all_gather(a, axis), part)
    state = jax.tree.map(lambda a, e: jnp.zeros_like(a) + jnp.asarray(e, a.dtype), part, identity)

    def one(step, state):
        source = count - 1 - step
        return combine(
            state, jax.tree.map(lambda a: lax.dynamic_index_in_dim(a, source, 0, False), gathered)
        )

    return lax.fori_loop(0, ahead, one, state)


def conv_act(padded, weight, resets, block):
    taps = weight.shape[1]
    length = padded.shape[1] - taps + 1
    position = jnp.arange(length) % block
    flags = jnp.repeat(resets.astype(jnp.float32), block)
    total = jnp.zeros((padded.shape[0], length, padded.shape[2]), jnp.float32)
    for tap_index in range(taps):
        valid = 1.0 - flags * (position < tap_index).astype(jnp.float32)
        offset = taps - 1 - tap_index
        total = (
            total
            + weight[:, tap_index][:, None, :]
            * padded[:, offset : offset + length]
            * valid[None, :, None]
        )
    return jax.nn.silu(total)


def features(activated, logits_decay, logits_write, rates, heads):
    length = activated.shape[1]
    size_key = activated.shape[2] // heads

    def unit(array):
        return array * lax.rsqrt(jnp.sum(array * array, axis=-1, keepdims=True) + 1e-06)

    queries = unit(activated[0].reshape(length, heads, size_key)) * size_key ** (-0.5)
    key_rows = unit(activated[1].reshape(length, heads, size_key))
    values = activated[2].reshape(length, heads, size_key)
    gate_log = -rates[None, :] * jax.nn.softplus(logits_decay)
    strength = jax.nn.sigmoid(logits_write)
    return (queries, key_rows, values, gate_log, strength)


def block_run(queries, key_rows, values, gate_log, strength, resets, initial, block):
    length, heads, size_key = queries.shape
    width_value = values.shape[-1]
    count = length // block

    def split(array):
        return array.reshape((count, block) + array.shape[1:])

    index = jnp.arange(block)
    strict = index[:, None] > index[None, :]
    inclusive = index[:, None] >= index[None, :]
    identity = jnp.eye(block, dtype=jnp.float32)

    def advance(state, inputs):
        query_blk, key_blk, value_blk, gate_blk, write_blk, reset_blk = inputs
        state = state * (1 - reset_blk).astype(jnp.float32)
        cumul = jnp.cumsum(gate_blk, axis=0).T
        spread = cumul[:, :, None] - cumul[:, None, :]
        lower_decay = jnp.where(strict, jnp.exp(jnp.where(strict, spread, 0.0)), 0.0)
        upper_decay = jnp.where(inclusive, jnp.exp(jnp.where(inclusive, spread, 0.0)), 0.0)
        writes = write_blk.T
        key_key = jnp.einsum("thd,shd->hts", key_blk, key_blk, precision=highest)
        system = lower_decay * key_key * writes[:, None, :] + identity
        growth = jnp.exp(cumul)
        key_state = jnp.einsum("thd,hvd->htv", key_blk, state, precision=highest)
        right_side = jnp.transpose(value_blk, (1, 0, 2)) - growth[:, :, None] * key_state
        deltas = lax.linalg.triangular_solve(
            system, right_side, left_side=True, lower=True, unit_diagonal=True
        )
        weighted = deltas * writes[:, :, None]
        query_key = jnp.einsum("thd,shd->hts", query_blk, key_blk, precision=highest)
        query_state = jnp.einsum("thd,hvd->htv", query_blk, state, precision=highest)
        mixed = growth[:, :, None] * query_state + jnp.einsum(
            "hts,hsv->htv", upper_decay * query_key, weighted, precision=highest
        )
        tail_decay = jnp.exp(cumul[:, -1:] - cumul)
        state = jnp.exp(cumul[:, -1])[:, None, None] * state + jnp.einsum(
            "hsv,shd->hvd", weighted * tail_decay[:, :, None], key_blk, precision=highest
        )
        return (state, jnp.transpose(mixed, (1, 0, 2)))

    final, outputs = lax.scan(
        jax.checkpoint(advance),
        initial,
        (split(queries), split(key_rows), split(values), split(gate_log), split(strength), resets),
    )
    return (outputs.reshape(length, heads, width_value), final)


def product(left, right):
    return jnp.einsum("hij,hjk->hik", left, right, precision=highest)


def combine(earlier, later):
    return (product(earlier[0], later[0]), product(earlier[1], later[0]) + later[1])


def body(
    q_raw,
    k_raw,
    v_raw,
    conv_weight,
    decay_logit,
    beta_logit,
    decay_rate,
    block_resets,
    norm_gain,
    d_out,
):
    tokens = q_raw.shape[1]
    width = q_raw.shape[2]
    heads = decay_logit.shape[2]
    size_head = width // heads
    edge_rows = conv_weight.shape[1] - 1
    full_width = width * lax.axis_size("head")
    arrived = shifted(
        (
            q_raw[0, tokens - edge_rows :],
            k_raw[0, tokens - edge_rows :],
            v_raw[0, tokens - edge_rows :],
        ),
        "ctx",
        1,
    )
    raw_rows = (q_raw[0], k_raw[0], v_raw[0])
    padded = jnp.stack(
        [jnp.concatenate([arrived[number], raw_rows[number]], 0) for number in range(3)]
    ).astype(jnp.float32)
    resets = block_resets[0]
    eye_heads = jnp.broadcast_to(
        jnp.eye(size_head, dtype=jnp.float32), (heads, size_head, size_head)
    )

    def local_pass(padded_in, weight, logits_decay, logits_write, rates):
        activated = conv_act(padded_in, weight, resets, BLOCK_LENGTH)
        queries, key_rows, values, gate_log, strength = features(
            activated, logits_decay, logits_write, rates, heads
        )
        values_wide = jnp.concatenate([values, jnp.zeros_like(values)], -1)
        initial = jnp.concatenate([jnp.zeros_like(eye_heads), eye_heads], 1)
        return block_run(
            queries, key_rows, values_wide, gate_log, strength, resets, initial, BLOCK_LENGTH
        )

    (wide_out, wide_state), pullback = jax.vjp(
        local_pass, padded, conv_weight, decay_logit[0], beta_logit[0], decay_rate
    )
    carry_q = wide_state[:, :size_head]
    carry_p = wide_state[:, size_head:]

    def pass_on(turn, carry):
        incoming = shifted(carry[1], "ctx", 1)
        return (incoming, product(incoming, carry_p) + carry_q)

    state_in = lax.fori_loop(
        0, lax.axis_size("ctx") - 1, pass_on, (jnp.zeros_like(carry_q), carry_q)
    )[0]
    reach_rows = wide_out[:, :, size_head:]
    mixed = wide_out[:, :, :size_head] + jnp.einsum(
        "thd,hvd->thv", reach_rows, state_in, precision=highest
    )
    flat_mix = mixed.reshape(tokens, width)
    total_sq = lax.psum(jnp.sum(flat_mix * flat_mix, axis=1), "head")
    row_scale = lax.rsqrt(total_sq / full_width + 1e-06)
    out = (flat_mix * row_scale[:, None] * norm_gain[None, :]).astype(jnp.bfloat16)[None]
    grad_y = d_out[0].astype(jnp.float32)
    weighted_grad = grad_y * norm_gain[None, :]
    dot_sum = lax.psum(jnp.sum(weighted_grad * flat_mix, axis=1), "head")
    grad_flat = (
        weighted_grad * row_scale[:, None]
        - flat_mix * (row_scale * row_scale * row_scale * dot_sum / full_width)[:, None]
    )
    grad_gain = jnp.sum(grad_y * flat_mix * row_scale[:, None], axis=0)
    grad_mixed = grad_flat.reshape(tokens, heads, size_head)
    grad_source = jnp.einsum("thv,thd->hvd", grad_mixed, reach_rows, precision=highest)
    transposed = jnp.transpose(carry_p, (0, 2, 1))
    state_grad = entering(
        (transposed, grad_source), "ctx", combine, (eye_heads, jnp.zeros_like(grad_source))
    )[1]
    grad_reach = jnp.einsum("thv,hvd->thd", grad_mixed, state_in, precision=highest)
    cot_out = jnp.concatenate([grad_mixed, grad_reach], -1)
    cot_state = jnp.concatenate(
        [state_grad, jnp.einsum("hvi,hvj->hij", state_in, state_grad, precision=highest)], 1
    )
    grad_pad, grad_conv, grad_decay, grad_beta, grad_rate = pullback((cot_out, cot_state))
    returned = shifted(grad_pad[:, :edge_rows].astype(jnp.bfloat16), "ctx", -1).astype(jnp.float32)
    grad_in = grad_pad[:, edge_rows:] + jnp.pad(returned, ((0, 0), (tokens - edge_rows, 0), (0, 0)))
    param_grads = lax.psum((grad_conv, grad_rate, grad_gain), ("dp", "ctx"))
    return (
        out,
        grad_in[0].astype(jnp.bfloat16)[None],
        grad_in[1].astype(jnp.bfloat16)[None],
        grad_in[2].astype(jnp.bfloat16)[None],
        param_grads[0],
        grad_decay[None],
        grad_beta[None],
        param_grads[1],
        param_grads[2],
    )


def solution(mesh):
    placed = (
        P("dp", "ctx", "head"),
        P("dp", "ctx", "head"),
        P("dp", "ctx", "head"),
        P(None, None, "head"),
        P("dp", "ctx", "head"),
        P("dp", "ctx", "head"),
        P("head"),
        P("dp", "ctx"),
        P("head"),
        P("dp", "ctx", "head"),
    )
    return jax.shard_map(
        body,
        mesh=mesh,
        in_specs=placed,
        out_specs=(
            P("dp", "ctx", "head"),
            P("dp", "ctx", "head"),
            P("dp", "ctx", "head"),
            P("dp", "ctx", "head"),
            P(None, None, "head"),
            P("dp", "ctx", "head"),
            P("dp", "ctx", "head"),
            P("head"),
            P("head"),
        ),
        check_vma=False,
    )
```

profile of v0, /device:TPU:0, one launch (start us, length us, event | category | flops | bytes accessed | tf_op | source)
XLA Modules:
  0.0 489.7 jit_solution(12554197799136400490)
XLA Ops:
  7.3 1.2 copy.327
  8.6 5.1 %collective-permute-start.1 = (bf16[3,1024]{0,1:T(8,128)(2,1)S(1)}, bf16[3,1024]{0,1:T(8,128)(2,1)S(1)}, u32[]{:S(2)}, u32[]{:S(2)}) collective-permute-start(bf16[3,1024]{0,1:T(8,128)(2,1)S(1)} %slice_bitcast_fusion.2), channel_id=1, source_target_pairs={{0,1},{1,2},{2,3},{4,5},{5,6},{6,7},{8,9},{9,10},{10,11},{12,13},{... | collective-permute-start | bytes 18440 | tf_op jit(solution)/shard_map/ppermute | solution.py:15
  13.7 1.1 copy.329
  14.9 3.5 collective-permute-start.2
  18.8 3.5 collective-permute-start.3
  26.1 4.3 collective-permute-done.3
  31.2 4.8 fusion.7
  38.6 1.2 fusion.19
  39.8 78.6 %custom-call.11 = f32[8,1,128,128]{2,3,1,0:T(8,128)S(1)} custom-call(f32[8,1,128,128]{3,2,1,0:T(8,128)S(1)} %fusion.19), custom_call_target="InvertDiagBlocksLowerTriangular" | custom-call | tf_op jit(solution)/shard_map/jvp()/while/body/eval_jaxpr/triangular_solve/custom-call.1 | solution.py:93
  120.6 2.2 convolution_add_fusion.2
  123.7 2.1 copy.350
  130.0 3.0 fusion.9
  133.0 78.1 %while.20 = (s32[]{:T(128)}, f32[8,128,128]{2,1,0:T(8,128)}, f32[8,128,128]{2,1,0:T(8,128)}, f32[8,128,128]{2,1,0:T(8,128)S(1)}, f32[8,128,128]{2,1,0:T(8,128)S(1)}) while((s32[]{:T(128)}, f32[8,128,128]{2,1,0:T(8,128)}, f32[8,128,128]{2,1,0:T(8,128)}, f32[8,128,128]{2,1,0:T(8,128)S(1)}, f32[8,128,128]{2,1,0:T(8,128)S(1)}) %tuple.129), condition=%wide.region_4.6_spmd.clone, body=%wide.region_3.5_spmd.sunk.clone | while | flops 201457664 | bytes 6291585 | solution.py:181
  133.0 4.4 collective-permute-start
  137.4 23.0 %collective-permute-done = f32[8,128,128]{2,1,0:T(8,128)S(1)} collective-permute-done((f32[8,128,128]{2,1,0:T(8,128)}, f32[8,128,128]{2,1,0:T(8,128)S(1)}, u32[]{:S(2)}, u32[]{:S(2)}) %collective-permute-start) | collective-permute-done | bytes 524320 | tf_op jit(solution)/shard_map/while/body/eval_jaxpr/ppermute | solution.py:15
  160.4 1.4 convolution_add_fusion.6
  161.9 13.5 %collective-permute-start = (f32[8,128,128]{2,1,0:T(8,128)}, f32[8,128,128]{2,1,0:T(8,128)S(1)}, u32[]{:S(2)}, u32[]{:S(2)}) collective-permute-start(f32[8,128,128]{2,1,0:T(8,128)} %get-tuple-element.581), channel_id=1, source_target_pairs={{0,1},{1,2},{2,3},{4,5},{5,6},{6,7},{8,9},{9,10},{10,11},{12,13},{... | collective-permute-start | bytes 1572872 | tf_op jit(solution)/shard_map/while/body/eval_jaxpr/ppermute | solution.py:15
  175.4 17.4 %collective-permute-done = f32[8,128,128]{2,1,0:T(8,128)S(1)} collective-permute-done((f32[8,128,128]{2,1,0:T(8,128)}, f32[8,128,128]{2,1,0:T(8,128)S(1)}, u32[]{:S(2)}, u32[]{:S(2)}) %collective-permute-start) | collective-permute-done | bytes 524320 | tf_op jit(solution)/shard_map/while/body/eval_jaxpr/ppermute | solution.py:15
  192.8 1.4 convolution_add_fusion.6
  194.2 4.3 collective-permute-start
  198.6 11.1 %collective-permute-done = f32[8,128,128]{2,1,0:T(8,128)S(1)} collective-permute-done((f32[8,128,128]{2,1,0:T(8,128)}, f32[8,128,128]{2,1,0:T(8,128)S(1)}, u32[]{:S(2)}, u32[]{:S(2)}) %collective-permute-start) | collective-permute-done | bytes 524320 | tf_op jit(solution)/shard_map/while/body/eval_jaxpr/ppermute | solution.py:15
  209.6 1.4 convolution_add_fusion.6
  211.1 2.1 multiply_reduce_fusion.13
  213.2 10.1 %psum.35 = f32[128]{0:T(128)S(1)} all-reduce(f32[128]{0:T(128)S(1)} %get-tuple-element.466), channel_id=1, replica_groups=mesh['dp'=2,'head'=4,'ctx'=4] {'head'}, use_global_device_ids=true, to_apply=%region_6.8 | all-reduce | flops 128 | bytes 1024 | tf_op jit(solution)/shard_map/psum | solution.py:189
  224.3 8.0 %psum.36 = f32[128]{0:T(128)S(1)} all-reduce(f32[128]{0:T(128)S(1)} %get-tuple-element.402), channel_id=1, replica_groups=mesh['dp'=2,'head'=4,'ctx'=4] {'head'}, use_global_device_ids=true, to_apply=%region_8.10 | all-reduce | flops 128 | bytes 1024 | tf_op jit(solution)/shard_map/psum | solution.py:194
  232.5 3.1 fusion.86
  237.1 2.1 concatenate.25
  243.2 39.3 %all-gather.7.cloned.1.call-done = f32[32,128,128]{2,1,0:T(8,128)} async-done(((f32[8,128,128]{2,1,0:T(8,128)}), f32[32,128,128]{2,1,0:T(8,128)}) %all-gather.7.cloned.1.call-update) | async-done | bytes 2097168 | tf_op jit(solution)/shard_map/all_gather | solution.py:22
  283.4 16.0 %while.21 = (s32[]{:T(128)}, f32[8,128,128]{1,2,0:T(8,128)}, s32[]{:T(128)}, f32[4,8,128,128]{3,2,1,0:T(8,128)}, f32[4,8,128,128]{3,2,1,0:T(8,128)}) while((s32[]{:T(128)}, f32[8,128,128]{1,2,0:T(8,128)}, s32[]{:T(128)}, f32[4,8,128,128]{3,2,1,0:T(8,128)}, f32[4,8,128,128]{3,2,1,0:T(8,128)}) %tuple.140), condition=%wide.region_10.12_spmd.clone, body=%wide.region_9.11_spmd.sunk.clone | while | flops 201457664 | bytes 5243003 | solution.py:31
  285.7 2.9 fusion.198
  290.9 2.9 fusion.198
  296.1 2.9 fusion.198
  299.4 1.2 copy.358
  300.6 2.2 fusion.146
  303.1 1.8 fusion.147
  305.0 2.1 fusion.148
  307.1 1.6 multiply_reduce_fusion.7
  308.7 1.8 fusion.149
  312.9 80.2 %custom-call.9 = f32[8,1,128,128]{2,3,1,0:T(8,128)} custom-call(f32[8,1,128,128]{3,2,1,0:T(8,128)} %add_bitcast_fusion), custom_call_target="InvertDiagBlocksLowerTriangular" | custom-call | tf_op jit(solution)/shard_map/transpose(jvp())/while/body/eval_jaxpr/checkpoint/triangular_solve | solution.py:93
  393.1 2.7 fusion.28
  395.8 1.3 convolution_add_fusion.1
  398.1 2.1 fusion.36
  400.3 2.5 copy.377
  402.8 2.5 multiply_reduce_fusion.5
  405.3 1.6 multiply_reduce_fusion.4
  407.0 2.8 fusion.25
  409.8 2.0 fusion.34
  412.6 2.1 copy.370
  416.1 2.0 multiply_reduce_fusion.9
  418.1 2.2 fusion.12
  420.3 1.9 fusion.13
  423.2 2.2 multiply_reduce_fusion.11
  425.5 2.2 multiply_reduce_fusion.10
  427.9 1.3 fusion.141
  429.3 1.1 reduce_window_sum.39
  430.7 1.3 add_add_fusion.1
  431.9 1.3 add_add_fusion
  433.3 3.1 multiply_reduce_fusion.3
  436.4 2.1 multiply_multiply_fusion.3
  438.5 2.5 pad_add_fusion
  441.0 1.6 copy-done.15
  443.1 1.3 collective-permute-start.4
  445.0 30.5 %all-reduce.16 = (f32[3,4,1024]{2,0,1:T(4,128)S(1)}, f32[8]{0:T(128)}, f32[1024]{0:T(1024)}) all-reduce(f32[3,4,1024]{2,0,1:T(4,128)S(1)} %pad_add_fusion.1, f32[8]{0:T(128)S(1)} %neg.53, f32[1024]{0:T(1024)S(1)} %bitcast.280), channel_id=1, replica_groups=mesh['dp'=2,'head'=4,'ctx'=4] {'dp','ctx'}, use_global_device_ids=true, to_apply=%region_18.20 | all-reduce | flops 13320 | bytes 106560 | tf_op jit(solution)/shard_map/psum | solution.py:214
  477.3 2.6 fusion.6
  (237 shorter events, 41.7 us)
Async XLA Ops:
  7.2 11.3 %copy-start.40 = (bf16[1,128,1024]{2,1,0:T(8,128)(2,1)S(1)}, bf16[1,128,1024]{2,1,0:T(8,128)(2,1)}, u32[]{:S(2)}) copy-start(bf16[1,128,1024]{2,1,0:T(8,128)(2,1)} %param.18) | copy-start | bytes 786436
  7.2 15.1 %copy-start.48 = (f32[1,128,8]{1,2,0:T(8,128)S(1)}, f32[1,128,8]{1,2,0:T(8,128)}, u32[]{:S(2)}) copy-start(f32[1,128,8]{1,2,0:T(8,128)} %param.20) | copy-start | bytes 12292
  7.2 15.9 %copy-start.63 = (f32[8]{0:T(128)S(1)}, f32[8]{0:T(128)}, u32[]{:S(2)}) copy-start(f32[8]{0:T(128)} %param.22) | copy-start | bytes 100
  7.2 15.9 %copy-start.49 = (f32[1,128,8]{1,2,0:T(8,128)S(1)}, f32[1,128,8]{1,2,0:T(8,128)}, u32[]{:S(2)}) copy-start(f32[1,128,8]{1,2,0:T(8,128)} %param.21) | copy-start | bytes 12292
  7.2 235.9 %all-gather.5.cloned.1.call-start = ((), (), s32[]{:S(2)}) async-start(), calls=%async_computation | async-start | bytes 2621440 | tf_op jit(solution)/shard_map/all_gather | solution.py:22
  8.4 15.0 %copy-start.42 = (f32[3,4,1024]{2,1,0:T(4,128)S(1)}, f32[3,4,1024]{2,1,0:T(4,128)}, u32[]{:S(2)}) copy-start(f32[3,4,1024]{2,1,0:T(4,128)} %param.19) | copy-start | bytes 147460
  8.6 15.6 %copy-start.39 = (bf16[1,128,1024]{2,1,0:T(8,128)(2,1)S(1)}, bf16[1,128,1024]{2,1,0:T(8,128)(2,1)}, u32[]{:S(2)}) copy-start(bf16[1,128,1024]{2,1,0:T(8,128)(2,1)} %param.25) | copy-start | bytes 786436
  8.6 16.6 %collective-permute-start.1 = (bf16[3,1024]{0,1:T(8,128)(2,1)S(1)}, bf16[3,1024]{0,1:T(8,128)(2,1)S(1)}, u32[]{:S(2)}, u32[]{:S(2)}) collective-permute-start(bf16[3,1024]{0,1:T(8,128)(2,1)S(1)} %slice_bitcast_fusion.2), channel_id=1, source_target_pairs={{0,1},{1,2},{2,3},{4,5},{5,6},{6,7},{8,9},{9,10},{10,11},{12,13},{... | collective-permute-start | bytes 18440 | tf_op jit(solution)/shard_map/ppermute | solution.py:15
  14.9 10.9 %collective-permute-start.2 = (bf16[3,1024]{0,1:T(8,128)(2,1)S(1)}, bf16[3,1024]{0,1:T(8,128)(2,1)S(1)}, u32[]{:S(2)}, u32[]{:S(2)}) collective-permute-start(bf16[3,1024]{0,1:T(8,128)(2,1)S(1)} %slice_bitcast_fusion.1), channel_id=1, source_target_pairs={{0,1},{1,2},{2,3},{4,5},{5,6},{6,7},{8,9},{9,10},{10,11},{12,13},{... | collective-permute-start | bytes 18440 | tf_op jit(solution)/shard_map/ppermute | solution.py:15
  18.8 11.7 %collective-permute-start.3 = (bf16[3,1024]{0,1:T(8,128)(2,1)S(1)}, bf16[3,1024]{0,1:T(8,128)(2,1)S(1)}, u32[]{:S(2)}, u32[]{:S(2)}) collective-permute-start(bf16[3,1024]{0,1:T(8,128)(2,1)S(1)} %slice_bitcast_fusion), channel_id=1, source_target_pairs={{0,1},{1,2},{2,3},{4,5},{5,6},{6,7},{8,9},{9,10},{10,11},{12,13},{... | collective-permute-start | bytes 18440 | tf_op jit(solution)/shard_map/ppermute | solution.py:15
  23.1 8.0 %copy-start.55 = (f32[128]{0:T(128)}, f32[128]{0:T(128)S(1)}, u32[]{:S(2)}) copy-start(f32[128]{0:T(128)S(1)} %get-tuple-element.476) | copy-start | bytes 1540
  23.2 8.0 %copy-start.57 = (f32[128]{0:T(128)}, f32[128]{0:T(128)S(1)}, u32[]{:S(2)}) copy-start(f32[128]{0:T(128)S(1)} %get-tuple-element.477) | copy-start | bytes 1540
  24.1 7.1 %copy-start.59 = (f32[128]{0:T(128)}, f32[128]{0:T(128)S(1)}, u32[]{:S(2)}) copy-start(f32[128]{0:T(128)S(1)} %get-tuple-element.474) | copy-start | bytes 1540
  24.1 7.1 %copy-start.61 = (f32[128]{0:T(128)}, f32[128]{0:T(128)S(1)}, u32[]{:S(2)}) copy-start(f32[128]{0:T(128)S(1)} %get-tuple-element.475) | copy-start | bytes 1540
  31.1 4.9 copy-start
  37.1 81.3 %copy-start.26 = (f32[1,128,1024]{1,2,0:T(8,128)}, f32[1,128,1024]{1,2,0:T(8,128)S(1)}, u32[]{:S(2)}) copy-start(f32[1,128,1024]{1,2,0:T(8,128)S(1)} %get-tuple-element.438) | copy-start | bytes 1572868
  37.2 81.2 %copy-start.44 = (f32[128,8]{0,1:T(8,128)}, f32[128,8]{0,1:T(8,128)S(1)}, u32[]{:S(2)}) copy-start(f32[128,8]{0,1:T(8,128)S(1)} %multiply_reduce_fusion.14) | copy-start | bytes 12292
  125.8 156.7 %all-gather.7.cloned.1.call-start = ((), (), s32[]{:S(2)}) async-start(), calls=%async_computation.1 | async-start | bytes 2621440 | tf_op jit(solution)/shard_map/all_gather | solution.py:22
  127.1 1.8 copy-start.5
  133.0 27.4 %collective-permute-start = (f32[8,128,128]{2,1,0:T(8,128)}, f32[8,128,128]{2,1,0:T(8,128)S(1)}, u32[]{:S(2)}, u32[]{:S(2)}) collective-permute-start(f32[8,128,128]{2,1,0:T(8,128)} %get-tuple-element.581), channel_id=1, source_target_pairs={{0,1},{1,2},{2,3},{4,5},{5,6},{6,7},{8,9},{9,10},{10,11},{12,13},{... | collective-permute-start | bytes 1572872 | tf_op jit(solution)/shard_map/while/body/eval_jaxpr/ppermute | solution.py:15
  161.9 30.9 %collective-permute-start = (f32[8,128,128]{2,1,0:T(8,128)}, f32[8,128,128]{2,1,0:T(8,128)S(1)}, u32[]{:S(2)}, u32[]{:S(2)}) collective-permute-start(f32[8,128,128]{2,1,0:T(8,128)} %get-tuple-element.581), channel_id=1, source_target_pairs={{0,1},{1,2},{2,3},{4,5},{5,6},{6,7},{8,9},{9,10},{10,11},{12,13},{... | collective-permute-start | bytes 1572872 | tf_op jit(solution)/shard_map/while/body/eval_jaxpr/ppermute | solution.py:15
  192.8 1.4 copy-start.2
  194.2 15.4 %collective-permute-start = (f32[8,128,128]{2,1,0:T(8,128)}, f32[8,128,128]{2,1,0:T(8,128)S(1)}, u32[]{:S(2)}, u32[]{:S(2)}) collective-permute-start(f32[8,128,128]{2,1,0:T(8,128)} %get-tuple-element.581), channel_id=1, source_target_pairs={{0,1},{1,2},{2,3},{4,5},{5,6},{6,7},{8,9},{9,10},{10,11},{12,13},{... | collective-permute-start | bytes 1572872 | tf_op jit(solution)/shard_map/while/body/eval_jaxpr/ppermute | solution.py:15
  209.6 1.4 copy-start.2
  211.1 12.3 %copy-start.25 = (f32[1,128,1024]{1,2,0:T(8,128)S(1)}, f32[1,128,1024]{1,2,0:T(8,128)}, u32[]{:S(2)}) copy-start(f32[1,128,1024]{1,2,0:T(8,128)} %copy.351) | copy-start | bytes 1572868
  211.1 12.3 %copy-start.43 = (f32[1024]{0:T(1024)S(1)}, f32[1024]{0:T(1024)}, u32[]{:S(2)}) copy-start(f32[1024]{0:T(1024)} %param.24) | copy-start | bytes 12292
  223.4 12.2 %copy-start.51 = (f32[128]{0:T(128)}, f32[128]{0:T(128)S(1)}, u32[]{:S(2)}) copy-start(f32[128]{0:T(128)S(1)} %add_rsqrt_fusion.2) | copy-start | bytes 1540
  235.7 4.6 copy-start.3
  240.2 2.1 copy-start.33
  240.3 2.1 copy-start.52
  302.9 2.1 copy-start.11
  307.1 1.6 copy-start.6
  307.1 3.5 copy-start.4
  393.1 2.7 copy-start.17
  393.1 2.7 copy-start.31
  395.8 2.3 copy-start.35
  402.8 2.5 copy-start.10
  402.8 2.5 copy-start.18
  402.8 2.5 copy-start.27
  402.8 2.5 copy-start.36
  407.0 4.8 copy-start.7
  409.8 2.0 copy-start.22
  411.8 2.9 copy-start.24
  412.6 2.9 copy-start.29
  416.0 2.0 copy-start.8
  416.0 2.0 copy-start.12
  418.1 2.2 copy-start.16
  423.2 2.2 copy-start.45
  423.2 2.2 copy-start.21
  423.2 2.2 copy-start.34
  423.2 2.2 copy-start.46
  425.5 5.1 %copy-start.41 = (pred[1,128,8]{2,1,0:T(8,128)(4,1)S(1)}, pred[1,128,8]{2,1,0:T(8,128)(4,1)}, u32[]{:S(2)}) copy-start(pred[1,128,8]{2,1,0:T(8,128)(4,1)} %copy.391) | copy-start | bytes 3076
  425.5 5.0 %copy-start.54 = (f32[8]{0:T(128)S(1)}, f32[8]{0:T(128)}, u32[]{:S(2)}) copy-start(f32[8]{0:T(128)} %copy-done.53) | copy-start | bytes 100
  425.5 7.7 %copy-start.23 = (f32[3,128,1024]{1,2,0:T(8,128)S(1)}, f32[3,128,1024]{1,2,0:T(8,128)}, u32[]{:S(2)}) copy-start(f32[3,128,1024]{1,2,0:T(8,128)} %get-tuple-element.432) | copy-start | bytes 4718596
  429.1 4.1 copy-start.30
  430.6 2.6 copy-start.1
  430.6 2.6 copy-start.56
  430.6 2.6 copy-start.58
  430.6 2.6 copy-start.60
  430.7 2.6 copy-start.62
  441.0 1.6 copy-start.15
  442.6 1.7 copy-start.50
  442.6 2.4 copy-start.47
  443.1 33.8 %collective-permute-start.4 = (bf16[3,3,1024]{2,1,0:T(4,128)(2,1)S(1)}, bf16[3,3,1024]{2,1,0:T(4,128)(2,1)S(1)}, u32[]{:S(2)}, u32[]{:S(2)}) collective-permute-start(bf16[3,3,1024]{2,1,0:T(4,128)(2,1)S(1)} %copy.382), channel_id=1, source_target_pairs={{1,0},{2,1},{3,2},{5,4},{6,5},{7,6},{9,8},{10,9},{11,10},{13,12},{... | collective-permute-start | bytes 55304 | tf_op jit(solution)/shard_map/ppermute | solution.py:15
  (11 other events, 12.7 us)
Sparse Core Ops, SparseCore 0:
  125.9 61.9 all-gather.4
  235.7 46.7 all-gather.6
where the time goes:
time: 499 us; the launch traced here: 490 us
  other arithmetic  190 us (38%)
  waiting for transfers between devices  95.7 us (19%)
  matrix products  65.7 us (13%)
  blocking collectives  48.6 us (10%)
  local copies, waits for them, and re-layouts  37.2 us (7%)
  starting transfers between devices  35.8 us (7%)
  between operations  16.2 us (3%)
    another operation x5, other arithmetic, advance(): lax.linalg.triangular_solve(system, right_side, left_side=True, lower=Tru...  160 us
    ppermute x7, waiting for transfers between devices, shifted(): lax.ppermute(value, axis, [(source, source + steps) for source in range(l...  56.3 us
    all_gather x2, waiting for transfers between devices, entering(): gathered = jax.tree.map(lambda a: lax.all_gather(a, axis), part)  39.3 us
    ppermute x7, starting transfers between devices, shifted(): lax.ppermute(value, axis, [(source, source + steps) for source in range(l...  35.5 us
    psum x1, blocking collectives, body(): param_grads = lax.psum((grad_conv, grad_rate, grad_gain), ('dp', 'ctx'))  30.5 us
    dot_general x6, matrix products, product(): return jnp.einsum('hij,hjk->hik', left, right, precision=highest)  12.9 us
    unnamed x138, local copies, waits for them, and re-layouts  12.6 us
    psum x1, blocking collectives, body(): total_sq = lax.psum(jnp.sum(flat_mix * flat_mix, axis=1), 'head')  10.1 us
  transfers between devices with their start and end apart: 9, of which 6 were waited for; matrix products, arithmetic and copies ran while one was open for 6% of the time, Pallas kernels for 0%

commit v1 on v0

v1 whole, which is shorter than its diff:
```python
import functools

import jax
import jax.numpy as jnp
from jax import lax
from jax.experimental import pallas as pl
from jax.experimental.pallas import tpu as pltpu
from jax.sharding import PartitionSpec as P

F32 = jnp.float32
BF16 = jnp.bfloat16
MESH = pl.DeviceIdType.MESH
VMEM_BYTES = 56 * 1024 * 1024
TILE = 16
EPS = 1e-06


def pair(x):
    hi = x.astype(BF16)
    return hi, (x - hi.astype(F32)).astype(BF16)


def dot_dims(a, b, dims):
    return lax.dot_general(a, b, (dims, ((), ())), preferred_element_type=F32)


def dot3(a, b, dims):
    return dot_dims(a[0], b[0], dims) + (dot_dims(a[0], b[1], dims) + dot_dims(a[1], b[0], dims))


NN = ((1,), (0,))
NT = ((1,), (1,))
TN = ((0,), (0,))


def iota(shape, dim):
    return lax.broadcasted_iota(jnp.int32, shape, dim)


def rows_sum(x):
    return jnp.sum(x, axis=1, keepdims=True)


def gates(logit, rate):
    soft = jnp.maximum(logit, 0.0) + jnp.log1p(jnp.exp(-jnp.abs(logit)))
    return soft, -rate * soft


def triple(x):
    hi, rest = pair(x)
    lo = (x - hi.astype(F32) - rest.astype(F32)).astype(BF16)
    return hi, rest, lo


def cumul_forms(gate):
    length = gate.shape[0]
    lower = (iota((length, length), 0) >= iota((length, length), 1)).astype(F32).astype(BF16)
    parts = triple(gate)
    col = sum(dot_dims(lower, p, NN) for p in parts)
    row = sum(dot_dims(p, lower, ((0,), (1,))) for p in parts)
    return col, row


def pick_col(x, lane):
    return rows_sum(jnp.where(iota(x.shape, 1) == lane, x, 0.0))


def pick_row(x, sub):
    return jnp.sum(jnp.where(iota(x.shape, 0) == sub, x, 0.0), axis=0, keepdims=True)


def greet(devices):
    barrier = pltpu.get_barrier_semaphore()
    for device in devices:
        pl.semaphore_signal(barrier, inc=1, device_id=device, device_id_type=MESH)
    pl.semaphore_wait(barrier, len(devices))


def ring_pair(count):
    place = lax.axis_index("ctx")
    return [{"ctx": lax.rem(place + 1, count)}, {"ctx": lax.rem(place + count - 1, count)}]


def others(axis, count):
    place = lax.axis_index(axis)
    return [{axis: lax.rem(place + step, count)} for step in range(1, count)]


def halo_kernel(count, q_ref, k_ref, v_ref, halo_ref, land, send_sem, recv_sem):
    place = lax.axis_index("ctx")
    tokens = q_ref.shape[0]
    greet(ring_pair(count))

    def copy(number, ref):
        return pltpu.make_async_remote_copy(
            src_ref=ref.at[pl.ds(tokens - TILE, TILE)],
            dst_ref=land.at[number],
            send_sem=send_sem.at[number],
            recv_sem=recv_sem.at[number],
            device_id={"ctx": lax.rem(place + 1, count)},
            device_id_type=MESH,
        )

    copies = [copy(number, ref) for number, ref in enumerate((q_ref, k_ref, v_ref))]

    @pl.when(place < count - 1)
    def _():
        for one in copies:
            one.start()

    @pl.when(place == 0)
    def _():
        halo_ref[...] = jnp.zeros_like(halo_ref)

    @pl.when(place > 0)
    def _():
        for one in copies:
            one.wait_recv()
        halo_ref[...] = land[...]

    @pl.when(place < count - 1)
    def _():
        for one in copies:
            one.wait_send()


def local_kernel(
    group,
    q_ref,
    k_ref,
    v_ref,
    halo_ref,
    conv_ref,
    decay_ref,
    beta_ref,
    rate_ref,
    reset_ref,
    y_ref,
    query_ref,
    key_ref,
    inv_ref,
    attn_ref,
    reach_key_ref,
    base_ref,
    reach_ref,
    mix_ref,
    carry_p_ref,
    carry_q_ref,
    padded,
):
    step = pl.program_id(0)
    length, width = q_ref.shape
    size = width // group
    taps = conv_ref.shape[1]
    keep = (1 - reset_ref[0, 0]).astype(F32)
    acts = []
    for number, ref in enumerate((q_ref, k_ref, v_ref)):
        padded[0:8, :] = halo_ref[number].astype(F32)[TILE - 8 :] * keep
        padded[8 : 8 + length, :] = ref[...].astype(F32)
        total = conv_ref[number, 0:1, :] * padded[8 : 8 + length, :]
        for tap in range(1, taps):
            total = total + conv_ref[number, tap : tap + 1, :] * padded[8 - tap : 8 - tap + length, :]
        y_ref[number] = total
        acts.append(total * jax.nn.sigmoid(total))
    gate = gates(decay_ref[...], rate_ref[...])[1]
    cumul_col, cumul_row = cumul_forms(gate)
    write_all = jax.nn.sigmoid(beta_ref[...])
    row_i = iota((length, length), 0)
    col_i = iota((length, length), 1)
    eye = (row_i == col_i).astype(F32)
    heads = range(group)
    state = []
    for j in heads:
        head = step * group + j
        cols = slice(j * size, (j + 1) * size)
        act_q, act_k, value = acts[0][:, cols], acts[1][:, cols], acts[2][:, cols]
        query = act_q * lax.rsqrt(rows_sum(act_q * act_q) + EPS) * size ** (-0.5)
        key = act_k * lax.rsqrt(rows_sum(act_k * act_k) + EPS)
        query_ref[j] = query
        key_ref[j] = key
        col = pick_col(cumul_col, head)
        row = pick_row(cumul_row, head)
        write = pick_col(write_all, head)
        spread = jnp.exp(jnp.minimum(col - row, 0.0))
        key_pair = pair(key)
        query_pair = pair(query)
        inner = dot3(key_pair, pair(write * key), NT)
        system = jnp.where(row_i > col_i, spread * inner, 0.0)
        attn = jnp.where(row_i >= col_i, spread * dot3(query_pair, key_pair, NT), 0.0)
        attn_ref[j] = attn
        state.append((key, query, value, col, write, system, attn, key_pair))
    inverse = [
        eye - jnp.where((row_i >> 1) == (col_i >> 1), state[j][5], 0.0) for j in heads
    ]
    level = 1
    while (2 << level) <= length:
        mask = ((row_i >> (level + 1)) == (col_i >> (level + 1))) & (
            (row_i >> level) != (col_i >> level)
        )
        pairs = [pair(inverse[j]) for j in heads]
        middle = [
            dot3(pairs[j], pair(jnp.where(mask, state[j][5], 0.0)), NN) for j in heads
        ]
        inverse = [inverse[j] - dot3(pair(middle[j]), pairs[j], NN) for j in heads]
        level += 1
    for j in heads:
        key, query, value, col, write, system, attn, key_pair = state[j]
        inv_ref[j] = inverse[j]
        inv_pair = pair(inverse[j])
        growth = jnp.exp(col)
        last = col[length - 1 : length, :]
        tail = jnp.exp(last - col)
        base = dot3(inv_pair, pair(value), NN)
        reach_key = dot3(inv_pair, pair(growth * key), NN)
        base_ref[j] = base
        reach_key_ref[j] = reach_key
        attn_pair = pair(attn)
        wide_base = write * base
        wide_reach = write * reach_key
        mix_ref[j] = dot3(attn_pair, pair(wide_base), NN)
        reach_ref[j] = keep * (growth * query - dot3(attn_pair, pair(wide_reach), NN))
        carry_q_ref[j] = dot3(pair(tail * wide_base), key_pair, TN)
        carry_p_ref[j] = keep * (
            jnp.exp(last) * eye - dot3(pair(tail * wide_reach), key_pair, TN)
        )


def chain_kernel(
    count,
    partners,
    mix_ref,
    reach_ref,
    carry_p_ref,
    carry_q_ref,
    d_out_ref,
    gain_ref,
    mixed_ref,
    stat_ref,
    state_ref,
    grad_ref,
    state_land,
    state_out,
    grad_land,
    grad_out,
    stat_land,
    state_send,
    state_recv,
    grad_send,
    grad_recv,
    stat_send,
    stat_recv,
):
    place = lax.axis_index("ctx")
    heads, length, size = mix_ref.shape
    full_width = heads * size * partners
    greet(ring_pair(count) + others("head", partners))

    def state_copy(h):
        return pltpu.make_async_remote_copy(
            src_ref=state_out.at[h],
            dst_ref=state_land.at[h],
            send_sem=state_send.at[h],
            recv_sem=state_recv.at[h],
            device_id={"ctx": lax.rem(place + 1, count)},
            device_id_type=MESH,
        )

    def grad_copy(h):
        return pltpu.make_async_remote_copy(
            src_ref=grad_out.at[h],
            dst_ref=grad_land.at[h],
            send_sem=grad_send.at[h],
            recv_sem=grad_recv.at[h],
            device_id={"ctx": lax.rem(place + count - 1, count)},
            device_id_type=MESH,
        )

    @pl.when(place == 0)
    def _():
        state_ref[...] = jnp.zeros_like(state_ref)

        def first(h, carry):
            state_out[h] = carry_q_ref[h]
            if count > 1:
                state_copy(h).start()
            return carry

        lax.fori_loop(0, heads, first, 0)

    @pl.when(place > 0)
    def _():
        def hop(h, carry):
            state_copy(h).wait_recv()
            entering = state_land[h]
            state_ref[h] = entering

            @pl.when(place < count - 1)
            def _():
                state_out[h] = carry_q_ref[h] + dot3(pair(entering), pair(carry_p_ref[h]), NN)
                state_copy(h).start()

            return carry

        lax.fori_loop(0, heads, hop, 0)

    def mixing(h, carry):
        square, inner = carry
        cols = pl.ds(pl.multiple_of(h * size, size), size)
        mixed = mix_ref[h] + dot3(pair(reach_ref[h]), pair(state_ref[h]), NT)
        mixed_ref[:, cols] = mixed
        weighted = d_out_ref[:, cols].astype(F32) * gain_ref[:, cols]
        return square + mixed * mixed, inner + weighted * mixed

    zero = jnp.zeros((length, size), F32)
    square, inner = lax.fori_loop(0, heads, mixing, (zero, zero))
    half = iota((length, size), 1) < size // 2
    mine = lax.axis_index("head")
    stat_land[mine] = jnp.where(half, rows_sum(square), rows_sum(inner))

    def stat_copy(target, slot):
        return pltpu.make_async_remote_copy(
            src_ref=stat_land.at[mine],
            dst_ref=stat_land.at[slot],
            send_sem=stat_send.at[target],
            recv_sem=stat_recv.at[slot],
            device_id={"head": target},
            device_id_type=MESH,
        )

    for step in range(1, partners):
        stat_copy(lax.rem(mine + step, partners), mine).start()
    for step in range(1, partners):
        source = lax.rem(mine + step, partners)
        stat_copy(source, source).wait_recv()
    stat = stat_land[0]
    for slot in range(1, partners):
        stat = stat + stat_land[slot]
    stat_ref[...] = stat
    scale = lax.rsqrt(stat[:, 0:1] / full_width + EPS)
    coef = scale * scale * scale * stat[:, size - 1 : size] / full_width

    def source_grad(h, carry):
        cols = pl.ds(pl.multiple_of(h * size, size), size)
        weighted = d_out_ref[:, cols].astype(F32) * gain_ref[:, cols]
        grad_mixed = weighted * scale - mixed_ref[:, cols] * coef
        grad_out[h] = dot3(pair(grad_mixed), pair(reach_ref[h]), TN)

        @pl.when((place == count - 1) & (place > 0))
        def _():
            grad_copy(h).start()

        return carry

    @pl.when(place > 0)
    def _():
        lax.fori_loop(0, heads, source_grad, 0)

    @pl.when(place == count - 1)
    def _():
        grad_ref[...] = jnp.zeros_like(grad_ref)

    @pl.when(place < count - 1)
    def _():
        def hop(h, carry):
            grad_copy(h).wait_recv()
            leaving = grad_land[h]
            grad_ref[h] = leaving

            @pl.when(place > 0)
            def _():
                grad_out[h] = grad_out[h] + dot3(pair(leaving), pair(carry_p_ref[h]), NT)
                grad_copy(h).start()

            return carry

        lax.fori_loop(0, heads, hop, 0)

    for step in range(1, partners):
        stat_copy(lax.rem(mine + step, partners), mine).wait_send()

    @pl.when(place < count - 1)
    def _():
        def done(h, carry):
            state_copy(h).wait_send()
            return carry

        lax.fori_loop(0, heads, done, 0)

    @pl.when(place > 0)
    def _():
        def done(h, carry):
            grad_copy(h).wait_send()
            return carry

        lax.fori_loop(0, heads, done, 0)


def back_kernel(
    group,
    full_width,
    q_ref,
    k_ref,
    v_ref,
    halo_ref,
    conv_ref,
    decay_ref,
    beta_ref,
    rate_ref,
    reset_ref,
    d_out_ref,
    gain_ref,
    mixed_ref,
    stat_ref,
    y_ref,
    query_ref,
    key_ref,
    inv_ref,
    attn_ref,
    reach_key_ref,
    base_ref,
    state_ref,
    grad_ref,
    out_ref,
    dq_ref,
    dk_ref,
    dv_ref,
    edge_ref,
    back_ref,
    param_ref,
    d_decay_ref,
    d_beta_ref,
    padded,
    d_conv,
):
    step = pl.program_id(0)
    length, width = q_ref.shape
    size = width // group
    taps = conv_ref.shape[1]
    keep = (1 - reset_ref[0, 0]).astype(F32)
    stat = stat_ref[...]
    scale = lax.rsqrt(stat[:, 0:1] / full_width + EPS)
    coef = scale * scale * scale * stat[:, size - 1 : size] / full_width
    mixed = mixed_ref[...]
    grad_y = d_out_ref[...].astype(F32)
    gain = gain_ref[...]
    normal = mixed * scale
    out_ref[...] = (normal * gain).astype(BF16)
    param_ref[...] = jnp.zeros_like(param_ref)
    param_ref[12:13, :] = jnp.sum(grad_y * normal, axis=0, keepdims=True)
    grad_mixed = grad_y * gain * scale - mixed * coef

    soft, gate = gates(decay_ref[...], rate_ref[...])
    slope = jax.nn.sigmoid(decay_ref[...])
    cumul_col, cumul_row = cumul_forms(gate)
    write_all = jax.nn.sigmoid(beta_ref[...])
    row_i = iota((length, length), 0)
    col_i = iota((length, length), 1)
    upper = (row_i <= col_i).astype(F32).astype(BF16)
    lanes = iota(decay_ref.shape, 1)

    @pl.when(step == 0)
    def _():
        d_decay_ref[...] = jnp.zeros_like(d_decay_ref)
        d_beta_ref[...] = jnp.zeros_like(d_beta_ref)

    heads = range(group)
    pre = []
    for j in heads:
        cols = slice(j * size, (j + 1) * size)
        head = step * group + j
        col = pick_col(cumul_col, head)
        row = pick_row(cumul_row, head)
        write = pick_col(write_all, head)
        spread = jnp.exp(jnp.minimum(col - row, 0.0))
        growth = jnp.exp(col)
        last = col[length - 1 : length, :]
        tail = jnp.exp(last - col)
        query, key = query_ref[j], key_ref[j]
        entering = keep * state_ref[j]
        leaving = grad_ref[j]
        enter_pair, leave_pair = pair(entering), pair(leaving)
        key_pair, query_pair = pair(key), pair(query)
        grad = grad_mixed[:, cols]
        grad_pair = pair(grad)
        delta = base_ref[j] - dot3(pair(reach_key_ref[j]), enter_pair, NT)
        used = write * delta
        used_pair = pair(used)
        d_used = dot3(pair(attn_ref[j]), grad_pair, TN) + tail * dot3(key_pair, leave_pair, NT)
        d_attn = jnp.where(row_i >= col_i, spread * dot3(grad_pair, used_pair, NT), 0.0)
        d_attn_pair = pair(d_attn)
        d_query = growth * dot3(grad_pair, enter_pair, NN) + dot3(d_attn_pair, key_pair, NN)
        d_key_tail = tail * dot3(used_pair, leave_pair, NN)
        d_key_plus = dot3(d_attn_pair, query_pair, TN) + d_key_tail
        right = dot3(pair(inv_ref[j]), pair(write * d_used), TN)
        right_pair = pair(right)
        d_system = jnp.where(row_i > col_i, -spread * dot3(right_pair, pair(delta), NT), 0.0)
        d_system_pair = pair(d_system)
        d_inner = dot3(d_system_pair, key_pair, TN)
        d_key_minus = dot3(d_system_pair, pair(write * key), NN) - growth * dot3(
            right_pair, enter_pair, NN
        )
        d_key_plus = d_key_plus + write * d_inner
        d_write = rows_sum(d_used * delta + key * d_inner)
        whole = jnp.sum(rows_sum(key * d_key_tail), axis=0, keepdims=True) + jnp.exp(
            last
        ) * jnp.sum(rows_sum(leaving * entering), axis=0, keepdims=True)
        d_cumul = rows_sum(query * d_query + key * (d_key_minus - d_key_plus))
        spot = jnp.where(iota(d_cumul.shape, 0) == length - 1, whole, 0.0)
        d_cumul = jnp.broadcast_to(d_cumul + spot, (length, size))
        d_gate = sum(dot_dims(upper, p, NN) for p in pair(d_cumul))[:, 0:1]
        d_key = d_key_plus + d_key_minus
        here = lanes == head
        d_decay_ref[...] += jnp.where(here, -rate_ref[...] * slope * d_gate, 0.0)
        d_beta_ref[...] += jnp.where(here, d_write * write_all * (1.0 - write_all), 0.0)
        d_rate = -jnp.sum(jnp.where(here, soft * d_gate, 0.0), keepdims=True)
        param_ref[13:14, cols] = jnp.broadcast_to(d_rate, (1, size))
        pre.append((d_query, d_key, right))

    rooted = size ** (-0.5)
    back_ref[...] = jnp.zeros_like(back_ref)
    for number, (ref, dst) in enumerate(((q_ref, dq_ref), (k_ref, dk_ref), (v_ref, dv_ref))):
        d_conv[0:8, :] = jnp.zeros((8, width), F32)
        d_conv[8 + length :, :] = jnp.zeros((8, width), F32)
        padded[0:8, :] = halo_ref[number].astype(F32)[TILE - 8 :] * keep
        padded[8 : 8 + length, :] = ref[...].astype(F32)
        for j in heads:
            cols = slice(j * size, (j + 1) * size)
            total = y_ref[number, :, cols]
            gated = jax.nn.sigmoid(total)
            grad = pre[j][number]
            if number < 2:
                act = total * gated
                inv_norm = lax.rsqrt(rows_sum(act * act) + EPS)
                unit = act * inv_norm
                if number == 0:
                    grad = grad * rooted
                grad = inv_norm * (grad - unit * rows_sum(unit * grad))
            d_conv[8 : 8 + length, cols] = grad * (gated * (1.0 + total * (1.0 - gated)))
        grad = d_conv[8 : 8 + length, :]
        extended = conv_ref[number, 0:1, :] * d_conv[0 : 8 + length, :]
        param_ref[4 * number : 4 * number + 1, :] = jnp.sum(
            grad * padded[8 : 8 + length, :], axis=0, keepdims=True
        )
        for tap in range(1, taps):
            extended = extended + conv_ref[number, tap : tap + 1, :] * d_conv[tap : tap + 8 + length, :]
            param_ref[4 * number + tap : 4 * number + tap + 1, :] = jnp.sum(
                grad * padded[8 - tap : 8 - tap + length, :], axis=0, keepdims=True
            )
        dst[...] = extended[8:].astype(BF16)
        edge_ref[8 * number : 8 * number + 8, :] = extended[length:]
        back_ref[8 * number : 8 * number + 8, :] = (keep * extended[0:8]).astype(BF16)


def sum_kernel(
    count,
    pairs,
    param_ref,
    back_ref,
    total_ref,
    arrived_ref,
    near_land,
    far_land,
    final_land,
    back_land,
    near_send,
    near_recv,
    far_send,
    far_recv,
    final_send,
    final_recv,
    back_send,
    back_recv,
):
    place = lax.axis_index("ctx")
    mine = lax.axis_index("dp")
    greet(others("ctx", count) + others("dp", pairs))

    back = pltpu.make_async_remote_copy(
        src_ref=back_ref,
        dst_ref=back_land,
        send_sem=back_send,
        recv_sem=back_recv,
        device_id={"ctx": lax.rem(place + count - 1, count)},
        device_id_type=MESH,
    )

    @pl.when(place > 0)
    def _():
        back.start()

    def near(target, slot):
        return pltpu.make_async_remote_copy(
            src_ref=param_ref.at[target],
            dst_ref=near_land.at[slot],
            send_sem=near_send.at[target],
            recv_sem=near_recv.at[slot],
            device_id={"dp": target},
            device_id_type=MESH,
        )

    def far(target, slot):
        return pltpu.make_async_remote_copy(
            src_ref=far_land.at[place],
            dst_ref=far_land.at[slot],
            send_sem=far_send.at[target],
            recv_sem=far_recv.at[slot],
            device_id={"ctx": target},
            device_id_type=MESH,
        )

    def final(target, slot):
        return pltpu.make_async_remote_copy(
            src_ref=final_land.at[mine],
            dst_ref=final_land.at[slot],
            send_sem=final_send.at[target],
            recv_sem=final_recv.at[slot],
            device_id={"dp": target},
            device_id_type=MESH,
        )

    def exchange(copy, here, total):
        for step in range(1, total):
            copy(lax.rem(here + step, total), here).start()
        for step in range(1, total):
            source = lax.rem(here + step, total)
            copy(source, source).wait_recv()

    def settle(copy, here, total):
        for step in range(1, total):
            copy(lax.rem(here + step, total), here).wait_send()

    near_land[mine] = param_ref[mine]
    exchange(near, mine, pairs)
    part = near_land[0]
    for slot in range(1, pairs):
        part = part + near_land[slot]
    far_land[place] = part
    exchange(far, place, count)
    part = far_land[0]
    for slot in range(1, count):
        part = part + far_land[slot]
    final_land[mine] = part
    exchange(final, mine, pairs)
    total_ref[...] = final_land[...]

    @pl.when(place == count - 1)
    def _():
        arrived_ref[...] = jnp.zeros_like(arrived_ref)

    @pl.when(place < count - 1)
    def _():
        back.wait_recv()
        arrived_ref[...] = back_land[...]

    settle(near, mine, pairs)
    settle(far, place, count)
    settle(final, mine, pairs)

    @pl.when(place > 0)
    def _():
        back.wait_send()


def remote_params(number):
    return pltpu.CompilerParams(
        collective_id=number, has_side_effects=True, vmem_limit_bytes=VMEM_BYTES
    )


def body(
    q_raw,
    k_raw,
    v_raw,
    conv_weight,
    decay_logit,
    beta_logit,
    decay_rate,
    block_resets,
    norm_gain,
    d_out,
):
    tokens, width = q_raw.shape[1:]
    heads = decay_logit.shape[2]
    size = width // heads
    taps = conv_weight.shape[1]
    count = lax.axis_size("ctx")
    partners = lax.axis_size("head")
    pairs = lax.axis_size("dp")
    group = 4 if heads % 4 == 0 else 1
    steps = heads // group
    span = group * size
    vmem = pl.BlockSpec(memory_space=pltpu.VMEM)
    shape = jax.ShapeDtypeStruct
    dma = pltpu.SemaphoreType.DMA
    raws = (q_raw[0], k_raw[0], v_raw[0])
    gain = norm_gain[None, :]
    rate = decay_rate[None, :]
    decay, beta = decay_logit[0], beta_logit[0]

    halo = pl.pallas_call(
        functools.partial(halo_kernel, count),
        out_shape=shape((3, TILE, width), BF16),
        in_specs=[pl.BlockSpec(memory_space=pl.ANY)] * 3,
        out_specs=vmem,
        scratch_shapes=[pltpu.VMEM((3, TILE, width), BF16), dma((3,)), dma((3,))],
        compiler_params=remote_params(0),
        name="halo",
    )(*raws)

    cols = pl.BlockSpec((tokens, span), lambda i: (0, i))
    halo_cols = pl.BlockSpec((3, TILE, span), lambda i: (0, 0, i))
    conv_cols = pl.BlockSpec((3, taps, span), lambda i: (0, 0, i))
    y_cols = pl.BlockSpec((3, tokens, span), lambda i: (0, 0, i))
    gate_all = pl.BlockSpec((tokens, heads), lambda i: (0, 0))
    rate_all = pl.BlockSpec((1, heads), lambda i: (0, 0))
    flag = pl.BlockSpec(memory_space=pltpu.SMEM)
    square = pl.BlockSpec((group, tokens, size), lambda i: (i, 0, 0))
    matrix = shape((heads, tokens, size), F32)
    local = pl.pallas_call(
        functools.partial(local_kernel, group),
        grid=(steps,),
        out_shape=[shape((3, tokens, width), F32)] + [matrix] * 10,
        in_specs=[cols] * 3 + [halo_cols, conv_cols, gate_all, gate_all, rate_all, flag],
        out_specs=[y_cols] + [square] * 10,
        scratch_shapes=[pltpu.VMEM((tokens + 8, span), F32)],
        compiler_params=pltpu.CompilerParams(vmem_limit_bytes=VMEM_BYTES),
        name="local",
    )(*raws, halo, conv_weight, decay, beta, rate, block_resets)
    y, query, key, inverse, attn, reach_key, base, reach, mix, carry_p, carry_q = local

    buffer = pltpu.VMEM((heads, size, size), F32)
    mixed, stat, state, grad = pl.pallas_call(
        functools.partial(chain_kernel, count, partners),
        out_shape=[
            shape((tokens, width), F32),
            shape((tokens, size), F32),
            shape((heads, size, size), F32),
            shape((heads, size, size), F32),
        ],
        in_specs=[vmem] * 6,
        out_specs=[vmem] * 4,
        scratch_shapes=[buffer] * 4
        + [pltpu.VMEM((partners, tokens, size), F32)]
        + [dma((heads,))] * 4
        + [dma((partners,))] * 2,
        compiler_params=remote_params(1),
        name="chain",
    )(mix, reach, carry_p, carry_q, d_out[0], gain)

    gain_cols = pl.BlockSpec((1, span), lambda i: (0, i))
    stat_all = pl.BlockSpec((tokens, size), lambda i: (0, 0))
    rows = lambda n: pl.BlockSpec((n, span), lambda i: (0, i))
    wide = shape((tokens, width), BF16)
    out, d_q, d_k, d_v, edge, back, param, d_decay, d_beta = pl.pallas_call(
        functools.partial(back_kernel, group, width * partners),
        grid=(steps,),
        out_shape=[wide] * 4
        + [
            shape((24, width), F32),
            shape((32, width), BF16),
            shape((16, width), F32),
            shape((tokens, heads), F32),
            shape((tokens, heads), F32),
        ],
        in_specs=[cols] * 3
        + [halo_cols, conv_cols, gate_all, gate_all, rate_all, flag]
        + [cols, gain_cols, cols, stat_all, y_cols]
        + [square] * 8,
        out_specs=[cols] * 4 + [rows(24), rows(32), rows(16), gate_all, gate_all],
        scratch_shapes=[
            pltpu.VMEM((tokens + 8, span), F32),
            pltpu.VMEM((tokens + 16, span), F32),
        ],
        compiler_params=pltpu.CompilerParams(vmem_limit_bytes=VMEM_BYTES),
        name="back",
    )(
        *raws, halo, conv_weight, decay, beta, rate, block_resets, d_out[0], gain, mixed, stat,
        y, query, key, inverse, attn, reach_key, base, state, grad,
    )

    rows_each = 16 // pairs
    total, arrived = pl.pallas_call(
        functools.partial(sum_kernel, count, pairs),
        out_shape=[shape((pairs, rows_each, width), F32), shape((32, width), BF16)],
        in_specs=[vmem] * 2,
        out_specs=[vmem] * 2,
        scratch_shapes=[
            pltpu.VMEM((pairs, rows_each, width), F32),
            pltpu.VMEM((count, rows_each, width), F32),
            pltpu.VMEM((pairs, rows_each, width), F32),
            pltpu.VMEM((32, width), BF16),
            dma((pairs,)),
            dma((pairs,)),
            dma((count,)),
            dma((count,)),
            dma((pairs,)),
            dma((pairs,)),
            dma,
            dma,
        ],
        compiler_params=remote_params(2),
        name="sums",
    )(param.reshape(pairs, rows_each, width), back)
    total = total.reshape(16, width)
    borrowed = taps - 1

    def finish(number, whole):
        come = arrived[8 * number + 8 - borrowed : 8 * number + 8].astype(F32)
        rows = (edge[8 * number + 8 - borrowed : 8 * number + 8] + come).astype(BF16)
        return lax.dynamic_update_slice(whole, rows, (tokens - borrowed, 0))[None]

    return (
        out[None],
        finish(0, d_q),
        finish(1, d_k),
        finish(2, d_v),
        total[:12].reshape(3, taps, width),
        d_decay[None],
        d_beta[None],
        total[13].reshape(heads, size)[:, 0],
        total[12],
    )


def solution(mesh):
    placed = (
        P("dp", "ctx", "head"),
        P("dp", "ctx", "head"),
        P("dp", "ctx", "head"),
        P(None, None, "head"),
        P("dp", "ctx", "head"),
        P("dp", "ctx", "head"),
        P("head"),
        P("dp", "ctx"),
        P("head"),
        P("dp", "ctx", "head"),
    )
    return jax.shard_map(
        body,
        mesh=mesh,
        in_specs=placed,
        out_specs=(
            P("dp", "ctx", "head"),
            P("dp", "ctx", "head"),
            P("dp", "ctx", "head"),
            P("dp", "ctx", "head"),
            P(None, None, "head"),
            P("dp", "ctx", "head"),
            P("dp", "ctx", "head"),
            P("head"),
            P("head"),
        ),
        check_vma=False,
    )
```

time: 499 us -> 108 us (0.22); the launches traced: 490 us -> 107 us
  other arithmetic: 190 us -> 0.84 us
  waiting for transfers between devices: 95.7 us -> 0 us
  Pallas kernels: 0 us -> 91.7 us
  matrix products: 65.7 us -> 0 us
  blocking collectives: 48.6 us -> 0 us
  starting transfers between devices: 35.8 us -> 0 us
  local copies, waits for them, and re-layouts: 37.2 us -> 13.4 us
  between operations: 16.2 us -> 1.33 us
    another operation x13 -> x0, other arithmetic: 165 us -> none  [the longest x5 160 us: advance(): lax.linalg.triangular_solve(system, right_side, left_side=True, lower=Tru...]
    pallas_call x0 -> x5, Pallas kernels: none -> 91.7 us  [the longest x1 48 us: body(): pl.pallas_call(functools.partial(chain_kernel, count, partners), out_shap...]
    dot_general x31 -> x0, matrix products: 58.8 us -> none  [the longest x6 12.9 us: product(): return jnp.einsum('hij,hjk->hik', left, right, precision=highest)]
    ppermute x7 -> x0, waiting for transfers between devices: 56.3 us -> none  [shifted(): lax.ppermute(value, axis, [(source, source + steps) for source in range(l...]
    psum x3 -> x0, blocking collectives: 48.6 us -> none  [the longest x1 30.5 us: body(): param_grads = lax.psum((grad_conv, grad_rate, grad_gain), ('dp', 'ctx'))]
    all_gather x2 -> x0, waiting for transfers between devices: 39.3 us -> none  [entering(): gathered = jax.tree.map(lambda a: lax.all_gather(a, axis), part)]
    ppermute x7 -> x0, starting transfers between devices: 35.5 us -> none  [shifted(): lax.ppermute(value, axis, [(source, source + steps) for source in range(l...]
    mul x11 -> x0, other arithmetic: 10.2 us -> none  [the longest x1 4.8 us: conv_act(): return jax.nn.silu(total)]
  transfers between devices with their start and end apart: 9 -> 0, of which waited for: 6 -> 0; matrix products, arithmetic and copies ran while one was open for 6% -> 0% of each run, Pallas kernels for 0% -> 0%
where the time goes in v1:
time: 108 us; the launch traced here: 107 us
  Pallas kernels  91.7 us (85%)
  local copies, waits for them, and re-layouts  13.4 us (12%)
  between operations  1.33 us (1%)
    pallas_call x1, Pallas kernels, body(): pl.pallas_call(functools.partial(chain_kernel, count, partners), out_shap...  48 us
    pallas_call x1, Pallas kernels, body(): pl.pallas_call(functools.partial(back_kernel, group, width * partners), g...  14.8 us
    pallas_call x1, Pallas kernels, body(): pl.pallas_call(functools.partial(local_kernel, group), grid=(steps,), out...  10.8 us
    pallas_call x1, Pallas kernels, body(): pl.pallas_call(functools.partial(sum_kernel, count, pairs), out_shape=[sh...  9.86 us
    pallas_call x1, Pallas kernels, body(): pl.pallas_call(functools.partial(halo_kernel, count), out_shape=shape((3,...  8.26 us
    unnamed x4, local copies, waits for them, and re-layouts  5.81 us
    dynamic_update_slice x3, local copies, waits for them, and re-layouts, finish(): return lax.dynamic_update_slice(whole, rows, (tokens - borrowed, 0))[None]  4.04 us

profile of v1, /device:TPU:0, one launch (start us, length us, event | category | flops | bytes accessed | tf_op | source)
XLA Modules:
  0.0 107.2 jit_solution(724765036909377993)
XLA Ops:
  1.3 1.4 %copy.27 = f32[1,128,8]{2,1,0:T(8,128)} copy(f32[1,128,8]{1,2,0:T(8,128)} %param.14) | data formatting | bytes 8192 | tf_op args[4]
  2.7 1.4 %copy.28 = f32[1,128,8]{2,1,0:T(8,128)} copy(f32[1,128,8]{1,2,0:T(8,128)} %param.15) | data formatting | bytes 8192 | tf_op args[5]
  4.1 8.3 %halo.1.halo_ref = bf16[3,16,1024]{2,1,0:T(8,128)(2,1)} custom-call(bf16[128,1024]{1,0:T(8,128)(2,1)} %bitcast.25, bf16[128,1024]{1,0:T(8,128)(2,1)} %bitcast.28, bf16[128,1024]{1,0:T(8,128)(2,1)} %bitcast.31), custom_call_target="tpu_custom_call" | custom-call | tf_op jit(solution)/shard_map/halo/pallas_call | solution.py:700
  12.4 10.8 %local.1 = (f32[3,128,1024]{2,1,0:T(8,128)}, f32[8,128,128]{2,1,0:T(8,128)}, f32[8,128,128]{2,1,0:T(8,128)}, f32[8,128,128]{2,1,0:T(8,128)}, f32[8,128,128]{2,1,...) custom-call(bf16[128,1024]{1,0:T(8,128)(2,1)} %bitcast.26, ...), custom_call_target="tpu_custom_call" | custom-call | tf_op jit(solution)/shard_map/local/pallas_call | solution.py:719
  23.2 48.0 %chain.1 = (f32[128,1024]{1,0:T(8,128)}, f32[128,128]{1,0:T(8,128)}, f32[8,128,128]{2,1,0:T(8,128)}, f32[8,128,128]{2,1,0:T(8,128)}) custom-call(f32[8,128,128]{2,1,0:T(8,128)} %get-tuple-element.35.mix_ref, f32[8,128,128]{2,1,0:T(8,128)} %get-tuple-element.36.reach_ref, f32[8,128,128]{2,1,0:T(8,128)} %get-tuple-element.37.carry_p_ref, ...), custom_call_target="tpu_custom_call" | custom-call | tf_op jit(solution)/shard_map/chain/pallas_call | solution.py:732
  71.1 14.8 %back.1 = (bf16[128,1024]{1,0:T(8,128)(2,1)}, bf16[128,1024]{1,0:T(8,128)(2,1)}, bf16[128,1024]{1,0:T(8,128)(2,1)}, bf16[128,1024]{1,0:T(8,128)(2,1)}, f32[24,10...) custom-call(bf16[128,1024]{1,0:T(8,128)(2,1)} %bitcast.27, ...), custom_call_target="tpu_custom_call" | custom-call | tf_op jit(solution)/shard_map/back/pallas_call | solution.py:754
  85.9 1.5 %copy.29 = f32[1,128,8]{1,2,0:T(8,128)} copy(f32[1,128,8]{2,1,0:T(8,128)} %bitcast.44) | data formatting | bytes 8192
  87.4 1.5 %copy.30 = f32[1,128,8]{1,2,0:T(8,128)} copy(f32[1,128,8]{2,1,0:T(8,128)} %bitcast.43) | data formatting | bytes 8192
  88.9 9.9 %sums.1 = (f32[2,8,1024]{2,1,0:T(8,128)}, bf16[32,1024]{1,0:T(8,128)(2,1)}) custom-call(f32[2,8,1024]{2,1,0:T(8,128)} %bitcast.42, bf16[32,1024]{1,0:T(8,128)(2,1)} %get-tuple-element.54.back_ref), custom_call_target="tpu_custom_call" | custom-call | tf_op jit(solution)/shard_map/sums/pallas_call | solution.py:782
  98.8 0.8 fusion.2
  99.6 1.4 %dynamic_update_slice.12 = bf16[1,128,1024]{2,1,0:T(8,128)(2,1)} dynamic-update-slice(bf16[1,128,1024]{2,1,0:T(8,128)(2,1)} %bitcast.54, bf16[1,3,1024]{2,1,0:T(4,128)(2,1)S(1)} %get-tuple-element.90, s32[]{:T(128)} %constant.5.clone.1, s32[]{:T(128)} %constant.6.clone.1, s32[]{:T(128)} %constant.5.clone.1) | dynamic-update-slice | bytes 12292 | tf_op jit(solution)/shard_map/dynamic_update_slice | solution.py:810
  101.0 1.3 %dynamic_update_slice.14 = bf16[1,128,1024]{2,1,0:T(8,128)(2,1)} dynamic-update-slice(bf16[1,128,1024]{2,1,0:T(8,128)(2,1)} %bitcast.53, bf16[1,3,1024]{2,1,0:T(4,128)(2,1)S(1)} %get-tuple-element.88, s32[]{:T(128)} %constant.5.clone.1, s32[]{:T(128)} %constant.6.clone.1, s32[]{:T(128)} %constant.5.clone.1) | dynamic-update-slice | bytes 12292 | tf_op jit(solution)/shard_map/dynamic_update_slice | solution.py:810
  102.3 1.3 %dynamic_update_slice.13 = bf16[1,128,1024]{2,1,0:T(8,128)(2,1)} dynamic-update-slice(bf16[1,128,1024]{2,1,0:T(8,128)(2,1)} %bitcast.52, bf16[1,3,1024]{2,1,0:T(4,128)(2,1)S(1)} %get-tuple-element.89, s32[]{:T(128)} %constant.5.clone.1, s32[]{:T(128)} %constant.6.clone.1, s32[]{:T(128)} %constant.5.clone.1) | dynamic-update-slice | bytes 12292 | tf_op jit(solution)/shard_map/dynamic_update_slice | solution.py:810
  103.7 1.4 %fusion.3 = (f32[1,1024]{1,0:T(1,128)}, f32[1,1024]{1,0:T(1,128)S(1)}) fusion(f32[16,1024]{1,0:T(8,128)} %bitcast.40), kind=kLoop, calls=%fused_computation.7 | loop fusion | bytes 16384 | tf_op jit(solution)/shard_map/slice | solution.py:821
  105.1 0.6 slice_reduce_fusion
  105.7 1.5 %reshape.35 = f32[3,4,1024]{2,1,0:T(4,128)} reshape(f32[12,1024]{1,0:T(8,128)} %bitcast.41) | data formatting | bytes 98304 | tf_op jit(solution)/shard_map/reshape | solution.py:817

commit v2 on v1

--- a/solution.py
+++ b/solution.py
@@ -53,11 +53,11 @@
 
 
 def cumul_forms(gate):
-    length = gate.shape[0]
+    length = gate.shape[1]
     lower = (iota((length, length), 0) >= iota((length, length), 1)).astype(F32).astype(BF16)
     parts = triple(gate)
-    col = sum(dot_dims(lower, p, NN) for p in parts)
-    row = sum(dot_dims(p, lower, ((0,), (1,))) for p in parts)
+    col = sum(dot_dims(lower, p, NT) for p in parts)
+    row = sum(dot_dims(p, lower, NT) for p in parts)
     return col, row
 
 
@@ -67,6 +67,12 @@
 
 def pick_row(x, sub):
     return jnp.sum(jnp.where(iota(x.shape, 0) == sub, x, 0.0), axis=0, keepdims=True)
+
+
+def column(row):
+    shape = (row.shape[1], row.shape[1])
+    spot = iota(shape, 0) == iota(shape, 1)
+    return rows_sum(jnp.where(spot, jnp.broadcast_to(row, shape), 0.0))
 
 
 def greet(devices):
@@ -162,7 +168,7 @@
             total = total + conv_ref[number, tap : tap + 1, :] * padded[8 - tap : 8 - tap + length, :]
         y_ref[number] = total
         acts.append(total * jax.nn.sigmoid(total))
-    gate = gates(decay_ref[...], rate_ref[...])[1]
+    gate = gates(decay_ref[...], column(rate_ref[...]))[1]
     cumul_col, cumul_row = cumul_forms(gate)
     write_all = jax.nn.sigmoid(beta_ref[...])
     row_i = iota((length, length), 0)
@@ -180,7 +186,7 @@
         key_ref[j] = key
         col = pick_col(cumul_col, head)
         row = pick_row(cumul_row, head)
-        write = pick_col(write_all, head)
+        write = column(pick_row(write_all, head))
         spread = jnp.exp(jnp.minimum(col - row, 0.0))
         key_pair = pair(key)
         query_pair = pair(query)
@@ -449,14 +455,16 @@
     param_ref[12:13, :] = jnp.sum(grad_y * normal, axis=0, keepdims=True)
     grad_mixed = grad_y * gain * scale - mixed * coef
 
-    soft, gate = gates(decay_ref[...], rate_ref[...])
+    rate = column(rate_ref[...])
+    soft, gate = gates(decay_ref[...], rate)
     slope = jax.nn.sigmoid(decay_ref[...])
     cumul_col, cumul_row = cumul_forms(gate)
     write_all = jax.nn.sigmoid(beta_ref[...])
     row_i = iota((length, length), 0)
     col_i = iota((length, length), 1)
     upper = (row_i <= col_i).astype(F32).astype(BF16)
-    lanes = iota(decay_ref.shape, 1)
+    gathered = jnp.zeros((length, size), F32)
+    half = size // 2
 
     @pl.when(step == 0)
     def _():
@@ -470,7 +478,7 @@
         head = step * group + j
         col = pick_col(cumul_col, head)
         row = pick_row(cumul_row, head)
-        write = pick_col(write_all, head)
+        write = column(pick_row(write_all, head))
         spread = jnp.exp(jnp.minimum(col - row, 0.0))
         growth = jnp.exp(col)
         last = col[length - 1 : length, :]
@@ -506,15 +514,20 @@
         ) * jnp.sum(rows_sum(leaving * entering), axis=0, keepdims=True)
         d_cumul = rows_sum(query * d_query + key * (d_key_minus - d_key_plus))
         spot = jnp.where(iota(d_cumul.shape, 0) == length - 1, whole, 0.0)
-        d_cumul = jnp.broadcast_to(d_cumul + spot, (length, size))
-        d_gate = sum(dot_dims(upper, p, NN) for p in pair(d_cumul))[:, 0:1]
         d_key = d_key_plus + d_key_minus
-        here = lanes == head
-        d_decay_ref[...] += jnp.where(here, -rate_ref[...] * slope * d_gate, 0.0)
-        d_beta_ref[...] += jnp.where(here, d_write * write_all * (1.0 - write_all), 0.0)
-        d_rate = -jnp.sum(jnp.where(here, soft * d_gate, 0.0), keepdims=True)
-        param_ref[13:14, cols] = jnp.broadcast_to(d_rate, (1, size))
+        gathered = gathered + jnp.where(col_i == head, d_cumul + spot, 0.0)
+        gathered = gathered + jnp.where(col_i == half + head, d_write, 0.0)
         pre.append((d_query, d_key, right))
+
+    turned = gathered.T
+    count = decay_ref.shape[0]
+    d_gate = sum(dot_dims(p, upper, NT) for p in pair(turned[0:count]))
+    d_decay_ref[...] += -rate * slope * d_gate
+    d_beta_ref[...] += turned[half : half + count] * write_all * (1.0 - write_all)
+    d_rate = -rows_sum(soft * d_gate)
+    for j in heads:
+        one = pick_row(d_rate, step * group + j)
+        param_ref[13:14, j * size : (j + 1) * size] = jnp.broadcast_to(one, (1, size))
 
     rooted = size ** (-0.5)
     back_ref[...] = jnp.zeros_like(back_ref)
@@ -659,6 +672,32 @@
     @pl.when(place > 0)
     def _():
         back.wait_send()
+
+
+def final_kernel(
+    q_ref, k_ref, v_ref, edge_ref, come_ref, total_ref, dq_ref, dk_ref, dv_ref, conv_ref, gain_ref, rate_ref
+):
+    length, width = q_ref.shape
+    numbers, taps = conv_ref.shape[:2]
+    heads = rate_ref.shape[1]
+    size = width // heads
+    for number, (ref, dst) in enumerate(((q_ref, dq_ref), (k_ref, dk_ref), (v_ref, dv_ref))):
+        dst[...] = ref[...]
+        part = slice(8 * number, 8 * number + 8)
+        rows = edge_ref[part, :] + jnp.where(
+            iota((8, width), 0) >= 9 - taps, come_ref[...].astype(F32)[part], 0.0
+        )
+        tile = jnp.concatenate([ref[length - TILE :, :].astype(F32)[0 : TILE - 8], rows], 0)
+        dst[length - TILE :, :] = tile.astype(BF16)
+    total = total_ref[...]
+    for number in range(numbers):
+        conv_ref[number] = total[number * taps : (number + 1) * taps]
+    gain_ref[...] = total[12:13]
+    rate = jnp.zeros(rate_ref.shape, F32)
+    for head in range(heads):
+        one = total[13:14, head * size : head * size + 1]
+        rate = rate + jnp.where(iota(rate.shape, 1) == head, one, 0.0)
+    rate_ref[...] = rate
 
 
 def remote_params(number):
@@ -695,7 +734,7 @@
     raws = (q_raw[0], k_raw[0], v_raw[0])
     gain = norm_gain[None, :]
     rate = decay_rate[None, :]
-    decay, beta = decay_logit[0], beta_logit[0]
+    decay, beta = decay_logit[0].T, beta_logit[0].T
 
     halo = pl.pallas_call(
         functools.partial(halo_kernel, count),
@@ -711,7 +750,7 @@
     halo_cols = pl.BlockSpec((3, TILE, span), lambda i: (0, 0, i))
     conv_cols = pl.BlockSpec((3, taps, span), lambda i: (0, 0, i))
     y_cols = pl.BlockSpec((3, tokens, span), lambda i: (0, 0, i))
-    gate_all = pl.BlockSpec((tokens, heads), lambda i: (0, 0))
+    gate_all = pl.BlockSpec((heads, tokens), lambda i: (0, 0))
     rate_all = pl.BlockSpec((1, heads), lambda i: (0, 0))
     flag = pl.BlockSpec(memory_space=pltpu.SMEM)
     square = pl.BlockSpec((group, tokens, size), lambda i: (i, 0, 0))
@@ -759,8 +798,8 @@
             shape((24, width), F32),
             shape((32, width), BF16),
             shape((16, width), F32),
-            shape((tokens, heads), F32),
-            shape((tokens, heads), F32),
+            shape((heads, tokens), F32),
+            shape((heads, tokens), F32),
         ],
         in_specs=[cols] * 3
         + [halo_cols, conv_cols, gate_all, gate_all, rate_all, flag]
@@ -802,23 +841,25 @@
         name="sums",
     )(param.reshape(pairs, rows_each, width), back)
     total = total.reshape(16, width)
-    borrowed = taps - 1
-
-    def finish(number, whole):
-        come = arrived[8 * number + 8 - borrowed : 8 * number + 8].astype(F32)
-        rows = (edge[8 * number + 8 - borrowed : 8 * number + 8] + come).astype(BF16)
-        return lax.dynamic_update_slice(whole, rows, (tokens - borrowed, 0))[None]
-
+    d_q, d_k, d_v, d_conv, d_gain, d_rate = pl.pallas_call(
+        final_kernel,
+        out_shape=[wide] * 3
+        + [shape((3, taps, width), F32), shape((1, width), F32), shape((1, heads), F32)],
+        in_specs=[vmem] * 6,
+        out_specs=[vmem] * 6,
+        compiler_params=pltpu.CompilerParams(vmem_limit_bytes=VMEM_BYTES),
+        name="final",
+    )(d_q, d_k, d_v, edge, arrived, total)
     return (
         out[None],
-        finish(0, d_q),
-        finish(1, d_k),
-        finish(2, d_v),
-        total[:12].reshape(3, taps, width),
-        d_decay[None],
-        d_beta[None],
-        total[13].reshape(heads, size)[:, 0],
-        total[12],
+        d_q[None],
+        d_k[None],
+        d_v[None],
+        d_conv,
+        d_decay.T[None],
+        d_beta.T[None],
+        d_rate[0],
+        d_gain[0],
     )
 
 

time: 108 us -> 94.3 us (0.87)
  local copies, waits for them, and re-layouts: 13.4 us -> 0 us
    unnamed x4 -> x0, local copies, waits for them, and re-layouts: 5.81 us -> none
    dynamic_update_slice x3 -> x0, local copies, waits for them, and re-layouts: 4.04 us -> none  [finish(): return lax.dynamic_update_slice(whole, rows, (tokens - borrowed, 0))[None]]
    pallas_call x0 -> x1, Pallas kernels: none -> 2.09 us  [body(): pl.pallas_call(final_kernel, out_shape=[wide] * 3 + [shape((3, taps, widt...]
    slice x2 -> x0, local copies, waits for them, and re-layouts: 2.06 us -> none  [the longest x1 1.43 us: body(): total[12]]
    reshape x1 -> x0, local copies, waits for them, and re-layouts: 1.47 us -> none  [body(): total[:12].reshape(3, taps, width)]
where the time goes in v2:
time: 94.3 us; the launch traced here: 94 us
  Pallas kernels  92.7 us (98%)
  between operations  1.32 us (1%)
    pallas_call x1, Pallas kernels, body(): pl.pallas_call(functools.partial(chain_kernel, count, partners), out_shap...  48 us
    pallas_call x1, Pallas kernels, body(): pl.pallas_call(functools.partial(back_kernel, group, width * partners), g...  13.8 us
    pallas_call x1, Pallas kernels, body(): pl.pallas_call(functools.partial(local_kernel, group), grid=(steps,), out...  10.6 us
    pallas_call x1, Pallas kernels, body(): pl.pallas_call(functools.partial(sum_kernel, count, pairs), out_shape=[sh...  9.89 us
    pallas_call x1, Pallas kernels, body(): pl.pallas_call(functools.partial(halo_kernel, count), out_shape=shape((3,...  8.31 us
    pallas_call x1, Pallas kernels, body(): pl.pallas_call(final_kernel, out_shape=[wide] * 3 + [shape((3, taps, widt...  2.09 us

profile of v2, /device:TPU:0, one launch (start us, length us, event | category | flops | bytes accessed | tf_op | source)
XLA Modules:
  0.0 94.0 jit_solution(11081821821117310407)
XLA Ops:
  1.3 8.3 %halo.1.halo_ref = bf16[3,16,1024]{2,1,0:T(8,128)(2,1)} custom-call(bf16[128,1024]{1,0:T(8,128)(2,1)} %bitcast.26, bf16[128,1024]{1,0:T(8,128)(2,1)} %bitcast.29, bf16[128,1024]{1,0:T(8,128)(2,1)} %bitcast.32), custom_call_target="tpu_custom_call" | custom-call | tf_op jit(solution)/shard_map/halo/pallas_call | solution.py:739
  9.6 10.6 %local.1 = (f32[3,128,1024]{2,1,0:T(8,128)}, f32[8,128,128]{2,1,0:T(8,128)}, f32[8,128,128]{2,1,0:T(8,128)}, f32[8,128,128]{2,1,0:T(8,128)}, f32[8,128,128]{2,1,...) custom-call(bf16[128,1024]{1,0:T(8,128)(2,1)} %bitcast.27, ...), custom_call_target="tpu_custom_call" | custom-call | tf_op jit(solution)/shard_map/local/pallas_call | solution.py:758
  20.2 48.0 %chain.1 = (f32[128,1024]{1,0:T(8,128)}, f32[128,128]{1,0:T(8,128)}, f32[8,128,128]{2,1,0:T(8,128)}, f32[8,128,128]{2,1,0:T(8,128)}) custom-call(f32[8,128,128]{2,1,0:T(8,128)} %get-tuple-element.41.mix_ref, f32[8,128,128]{2,1,0:T(8,128)} %get-tuple-element.42.reach_ref, f32[8,128,128]{2,1,0:T(8,128)} %get-tuple-element.43.carry_p_ref, ...), custom_call_target="tpu_custom_call" | custom-call | tf_op jit(solution)/shard_map/chain/pallas_call | solution.py:771
  68.3 13.8 %back.1 = (bf16[128,1024]{1,0:T(8,128)(2,1)}, bf16[128,1024]{1,0:T(8,128)(2,1)}, bf16[128,1024]{1,0:T(8,128)(2,1)}, bf16[128,1024]{1,0:T(8,128)(2,1)}, f32[24,10...) custom-call(bf16[128,1024]{1,0:T(8,128)(2,1)} %bitcast.28, ...), custom_call_target="tpu_custom_call" | custom-call | tf_op jit(solution)/shard_map/back/pallas_call | solution.py:793
  82.1 9.9 %sums.1 = (f32[2,8,1024]{2,1,0:T(8,128)}, bf16[32,1024]{1,0:T(8,128)(2,1)}) custom-call(f32[2,8,1024]{2,1,0:T(8,128)} %bitcast.38, bf16[32,1024]{1,0:T(8,128)(2,1)} %get-tuple-element.62.back_ref), custom_call_target="tpu_custom_call" | custom-call | tf_op jit(solution)/shard_map/sums/pallas_call | solution.py:821
  92.0 2.1 %final.1 = (bf16[128,1024]{1,0:T(8,128)(2,1)}, bf16[128,1024]{1,0:T(8,128)(2,1)}, bf16[128,1024]{1,0:T(8,128)(2,1)}, f32[3,4,1024]{2,1,0:T(4,128)}, f32[1,1024]{1,0:T(1,128)}, /*index=5*/f32[1,8]{1,0:T(1,128)}) custom-call(bf16[128,1024]{1,0:T(8,128)(2,1)} %get-tuple-element.57.q_ref, bf16[128,1024]{1,0:T(8,128)(2,1)} %get-tuple-element.58.k_ref, ...), custom_call_target="tpu_custom_call" | custom-call | tf_op jit(solution)/shard_map/final/pallas_call | solution.py:844

commit v3 on v2

--- a/solution.py
+++ b/solution.py
@@ -92,45 +92,8 @@
     return [{axis: lax.rem(place + step, count)} for step in range(1, count)]
 
 
-def halo_kernel(count, q_ref, k_ref, v_ref, halo_ref, land, send_sem, recv_sem):
-    place = lax.axis_index("ctx")
-    tokens = q_ref.shape[0]
-    greet(ring_pair(count))
-
-    def copy(number, ref):
-        return pltpu.make_async_remote_copy(
-            src_ref=ref.at[pl.ds(tokens - TILE, TILE)],
-            dst_ref=land.at[number],
-            send_sem=send_sem.at[number],
-            recv_sem=recv_sem.at[number],
-            device_id={"ctx": lax.rem(place + 1, count)},
-            device_id_type=MESH,
-        )
-
-    copies = [copy(number, ref) for number, ref in enumerate((q_ref, k_ref, v_ref))]
-
-    @pl.when(place < count - 1)
-    def _():
-        for one in copies:
-            one.start()
-
-    @pl.when(place == 0)
-    def _():
-        halo_ref[...] = jnp.zeros_like(halo_ref)
-
-    @pl.when(place > 0)
-    def _():
-        for one in copies:
-            one.wait_recv()
-        halo_ref[...] = land[...]
-
-    @pl.when(place < count - 1)
-    def _():
-        for one in copies:
-            one.wait_send()
-
-
-def local_kernel(
+def local_part(
+    step,
     group,
     q_ref,
     k_ref,
@@ -154,7 +117,6 @@
     carry_q_ref,
     padded,
 ):
-    step = pl.program_id(0)
     length, width = q_ref.shape
     size = width // group
     taps = conv_ref.shape[1]
@@ -231,177 +193,8 @@
         )
 
 
-def chain_kernel(
-    count,
-    partners,
-    mix_ref,
-    reach_ref,
-    carry_p_ref,
-    carry_q_ref,
-    d_out_ref,
-    gain_ref,
-    mixed_ref,
-    stat_ref,
-    state_ref,
-    grad_ref,
-    state_land,
-    state_out,
-    grad_land,
-    grad_out,
-    stat_land,
-    state_send,
-    state_recv,
-    grad_send,
-    grad_recv,
-    stat_send,
-    stat_recv,
-):
-    place = lax.axis_index("ctx")
-    heads, length, size = mix_ref.shape
-    full_width = heads * size * partners
-    greet(ring_pair(count) + others("head", partners))
-
-    def state_copy(h):
-        return pltpu.make_async_remote_copy(
-            src_ref=state_out.at[h],
-            dst_ref=state_land.at[h],
-            send_sem=state_send.at[h],
-            recv_sem=state_recv.at[h],
-            device_id={"ctx": lax.rem(place + 1, count)},
-            device_id_type=MESH,
-        )
-
-    def grad_copy(h):
-        return pltpu.make_async_remote_copy(
-            src_ref=grad_out.at[h],
-            dst_ref=grad_land.at[h],
-            send_sem=grad_send.at[h],
-            recv_sem=grad_recv.at[h],
-            device_id={"ctx": lax.rem(place + count - 1, count)},
-            device_id_type=MESH,
-        )
-
-    @pl.when(place == 0)
-    def _():
-        state_ref[...] = jnp.zeros_like(state_ref)
-
-        def first(h, carry):
-            state_out[h] = carry_q_ref[h]
-            if count > 1:
-                state_copy(h).start()
-            return carry
-
-        lax.fori_loop(0, heads, first, 0)
-
-    @pl.when(place > 0)
-    def _():
-        def hop(h, carry):
-            state_copy(h).wait_recv()
-            entering = state_land[h]
-            state_ref[h] = entering
-
-            @pl.when(place < count - 1)
-            def _():
-                state_out[h] = carry_q_ref[h] + dot3(pair(entering), pair(carry_p_ref[h]), NN)
-                state_copy(h).start()
-
-            return carry
-
-        lax.fori_loop(0, heads, hop, 0)
-
-    def mixing(h, carry):
-        square, inner = carry
-        cols = pl.ds(pl.multiple_of(h * size, size), size)
-        mixed = mix_ref[h] + dot3(pair(reach_ref[h]), pair(state_ref[h]), NT)
-        mixed_ref[:, cols] = mixed
-        weighted = d_out_ref[:, cols].astype(F32) * gain_ref[:, cols]
-        return square + mixed * mixed, inner + weighted * mixed
-
-    zero = jnp.zeros((length, size), F32)
-    square, inner = lax.fori_loop(0, heads, mixing, (zero, zero))
-    half = iota((length, size), 1) < size // 2
-    mine = lax.axis_index("head")
-    stat_land[mine] = jnp.where(half, rows_sum(square), rows_sum(inner))
-
-    def stat_copy(target, slot):
-        return pltpu.make_async_remote_copy(
-            src_ref=stat_land.at[mine],
-            dst_ref=stat_land.at[slot],
-            send_sem=stat_send.at[target],
-            recv_sem=stat_recv.at[slot],
-            device_id={"head": target},
-            device_id_type=MESH,
-        )
-
-    for step in range(1, partners):
-        stat_copy(lax.rem(mine + step, partners), mine).start()
-    for step in range(1, partners):
-        source = lax.rem(mine + step, partners)
-        stat_copy(source, source).wait_recv()
-    stat = stat_land[0]
-    for slot in range(1, partners):
-        stat = stat + stat_land[slot]
-    stat_ref[...] = stat
-    scale = lax.rsqrt(stat[:, 0:1] / full_width + EPS)
-    coef = scale * scale * scale * stat[:, size - 1 : size] / full_width
-
-    def source_grad(h, carry):
-        cols = pl.ds(pl.multiple_of(h * size, size), size)
-        weighted = d_out_ref[:, cols].astype(F32) * gain_ref[:, cols]
-        grad_mixed = weighted * scale - mixed_ref[:, cols] * coef
-        grad_out[h] = dot3(pair(grad_mixed), pair(reach_ref[h]), TN)
-
-        @pl.when((place == count - 1) & (place > 0))
-        def _():
-            grad_copy(h).start()
-
-        return carry
-
-    @pl.when(place > 0)
-    def _():
-        lax.fori_loop(0, heads, source_grad, 0)
-
-    @pl.when(place == count - 1)
-    def _():
-        grad_ref[...] = jnp.zeros_like(grad_ref)
-
-    @pl.when(place < count - 1)
-    def _():
-        def hop(h, carry):
-            grad_copy(h).wait_recv()
-            leaving = grad_land[h]
-            grad_ref[h] = leaving
-
-            @pl.when(place > 0)
-            def _():
-                grad_out[h] = grad_out[h] + dot3(pair(leaving), pair(carry_p_ref[h]), NT)
-                grad_copy(h).start()
-
-            return carry
-
-        lax.fori_loop(0, heads, hop, 0)
-
-    for step in range(1, partners):
-        stat_copy(lax.rem(mine + step, partners), mine).wait_send()
-
-    @pl.when(place < count - 1)
-    def _():
-        def done(h, carry):
-            state_copy(h).wait_send()
-            return carry
-
-        lax.fori_loop(0, heads, done, 0)
-
-    @pl.when(place > 0)
-    def _():
-        def done(h, carry):
-            grad_copy(h).wait_send()
-            return carry
-
-        lax.fori_loop(0, heads, done, 0)
-
-
-def back_kernel(
+def back_part(
+    step,
     group,
     full_width,
     q_ref,
@@ -438,7 +231,6 @@
     padded,
     d_conv,
 ):
-    step = pl.program_id(0)
     length, width = q_ref.shape
     size = width // group
     taps = conv_ref.shape[1]
@@ -564,17 +356,68 @@
         back_ref[8 * number : 8 * number + 8, :] = (keep * extended[0:8]).astype(BF16)
 
 
-def sum_kernel(
+def mixer_kernel(
     count,
+    partners,
     pairs,
-    param_ref,
-    back_ref,
+    group,
+    q_ref,
+    k_ref,
+    v_ref,
+    conv_ref,
+    decay_ref,
+    beta_ref,
+    rate_ref,
+    reset_ref,
+    d_out_ref,
+    gain_ref,
+    out_ref,
+    dq_ref,
+    dk_ref,
+    dv_ref,
+    edge_ref,
+    d_decay_ref,
+    d_beta_ref,
     total_ref,
     arrived_ref,
+    y_ref,
+    query_ref,
+    key_ref,
+    inv_ref,
+    attn_ref,
+    reach_key_ref,
+    base_ref,
+    reach_ref,
+    mix_ref,
+    carry_p_ref,
+    carry_q_ref,
+    state_ref,
+    grad_ref,
+    state_land,
+    state_out,
+    grad_land,
+    grad_out,
+    mixed_ref,
+    stat_ref,
+    stat_land,
+    halo_ref,
+    halo_land,
+    back_ref,
+    back_land,
+    param_ref,
     near_land,
     far_land,
     final_land,
-    back_land,
+    padded,
+    d_conv,
+    halo_send,
+    halo_recv,
+    state_send,
+    state_recv,
+    grad_send,
+    grad_recv,
+    stat_send,
+    stat_recv,
     near_send,
     near_recv,
     far_send,
@@ -585,8 +428,238 @@
     back_recv,
 ):
     place = lax.axis_index("ctx")
-    mine = lax.axis_index("dp")
-    greet(others("ctx", count) + others("dp", pairs))
+    core = lax.axis_index("dp")
+    heads, length, size = mix_ref.shape
+    steps = heads // group
+    span = group * size
+    rows = param_ref.shape[0] // pairs
+    full_width = heads * size * partners
+    raws = (q_ref, k_ref, v_ref)
+    kept = (query_ref, key_ref, inv_ref, attn_ref, reach_key_ref, base_ref)
+    greet(others("ctx", count) + others("head", partners) + others("dp", pairs))
+
+    def halo_copy(number):
+        return pltpu.make_async_remote_copy(
+            src_ref=raws[number].at[pl.ds(length - TILE, TILE)],
+            dst_ref=halo_land.at[number],
+            send_sem=halo_send.at[number],
+            recv_sem=halo_recv.at[number],
+            device_id={"ctx": lax.rem(place + 1, count)},
+            device_id_type=MESH,
+        )
+
+    @pl.when(place < count - 1)
+    def _():
+        for number in range(3):
+            halo_copy(number).start()
+
+    @pl.when(place == 0)
+    def _():
+        halo_ref[...] = jnp.zeros_like(halo_ref)
+
+    @pl.when(place > 0)
+    def _():
+        for number in range(3):
+            halo_copy(number).wait_recv()
+        halo_ref[...] = halo_land[...]
+
+    @pl.when(place < count - 1)
+    def _():
+        for number in range(3):
+            halo_copy(number).wait_send()
+
+    def state_copy(h):
+        return pltpu.make_async_remote_copy(
+            src_ref=state_out.at[h],
+            dst_ref=state_land.at[h],
+            send_sem=state_send.at[h],
+            recv_sem=state_recv.at[h],
+            device_id={"ctx": lax.rem(place + 1, count)},
+            device_id_type=MESH,
+        )
+
+    def grad_copy(h):
+        return pltpu.make_async_remote_copy(
+            src_ref=grad_out.at[h],
+            dst_ref=grad_land.at[h],
+            send_sem=grad_send.at[h],
+            recv_sem=grad_recv.at[h],
+            device_id={"ctx": lax.rem(place + count - 1, count)},
+            device_id_type=MESH,
+        )
+
+    def forward(step, carry):
+        wide = pl.ds(pl.multiple_of(step * span, span), span)
+        some = pl.ds(step * group, group)
+        local_part(
+            step,
+            group,
+            *[ref.at[:, wide] for ref in raws],
+            halo_ref.at[:, :, wide],
+            conv_ref.at[:, :, wide],
+            decay_ref,
+            beta_ref,
+            rate_ref,
+            reset_ref,
+            y_ref.at[:, :, wide],
+            *[ref.at[some] for ref in (*kept, reach_ref, mix_ref, carry_p_ref, carry_q_ref)],
+            padded,
+        )
+
+        @pl.when(place == 0)
+        def _():
+            for j in range(group):
+                h = step * group + j
+                state_ref[h] = jnp.zeros((size, size), F32)
+                state_out[h] = carry_q_ref[h]
+                if count > 1:
+                    state_copy(h).start()
+
+        return carry
+
+    lax.fori_loop(0, steps, forward, 0)
+
+    @pl.when(place > 0)
+    def _():
+        def hop(h, carry):
+            state_copy(h).wait_recv()
+            entering = state_land[h]
+            state_ref[h] = entering
+
+            @pl.when(place < count - 1)
+            def _():
+                state_out[h] = carry_q_ref[h] + dot3(pair(entering), pair(carry_p_ref[h]), NN)
+                state_copy(h).start()
+
+            return carry
+
+        lax.fori_loop(0, heads, hop, 0)
+
+    def mixing(h, carry):
+        square, inner = carry
+        cols = pl.ds(pl.multiple_of(h * size, size), size)
+        mixed = mix_ref[h] + dot3(pair(reach_ref[h]), pair(state_ref[h]), NT)
+        mixed_ref[:, cols] = mixed
+        weighted = d_out_ref[:, cols].astype(F32) * gain_ref[:, cols]
+        return square + mixed * mixed, inner + weighted * mixed
+
+    zero = jnp.zeros((length, size), F32)
+    square, inner = lax.fori_loop(0, heads, mixing, (zero, zero))
+    half = iota((length, size), 1) < size // 2
+    mine = lax.axis_index("head")
+    stat_land[mine] = jnp.where(half, rows_sum(square), rows_sum(inner))
+
+    def stat_copy(target, slot):
+        return pltpu.make_async_remote_copy(
+            src_ref=stat_land.at[mine],
+            dst_ref=stat_land.at[slot],
+            send_sem=stat_send.at[target],
+            recv_sem=stat_recv.at[slot],
+            device_id={"head": target},
+            device_id_type=MESH,
+        )
+
+    for step in range(1, partners):
+        stat_copy(lax.rem(mine + step, partners), mine).start()
+    for step in range(1, partners):
+        source = lax.rem(mine + step, partners)
+        stat_copy(source, source).wait_recv()
+    stat = stat_land[0]
+    for slot in range(1, partners):
+        stat = stat + stat_land[slot]
+    stat_ref[...] = stat
+    scale = lax.rsqrt(stat[:, 0:1] / full_width + EPS)
+    coef = scale * scale * scale * stat[:, size - 1 : size] / full_width
+
+    def source_grad(h, carry):
+        cols = pl.ds(pl.multiple_of(h * size, size), size)
+        weighted = d_out_ref[:, cols].astype(F32) * gain_ref[:, cols]
+        grad_mixed = weighted * scale - mixed_ref[:, cols] * coef
+        grad_out[h] = dot3(pair(grad_mixed), pair(reach_ref[h]), TN)
+
+        @pl.when((place == count - 1) & (place > 0))
+        def _():
+            grad_copy(h).start()
+
+        return carry
+
+    @pl.when(place > 0)
+    def _():
+        lax.fori_loop(0, heads, source_grad, 0)
+
+    @pl.when(place == count - 1)
+    def _():
+        grad_ref[...] = jnp.zeros_like(grad_ref)
+
+    def hop(h, carry):
+        grad_copy(h).wait_recv()
+        leaving = grad_land[h]
+        grad_ref[h] = leaving
+
+        @pl.when(place > 0)
+        def _():
+            grad_out[h] = grad_out[h] + dot3(pair(leaving), pair(carry_p_ref[h]), NT)
+            grad_copy(h).start()
+
+        return carry
+
+    def backward(step, carry):
+        wide = pl.ds(pl.multiple_of(step * span, span), span)
+        some = pl.ds(step * group, group)
+
+        @pl.when((place < count - 1) & (place > 0) & (step == 0))
+        def _():
+            lax.fori_loop(0, heads, hop, 0)
+
+        @pl.when((place < count - 1) & (place == 0))
+        def _():
+            lax.fori_loop(step * group, step * group + group, hop, 0)
+
+        back_part(
+            step,
+            group,
+            full_width,
+            *[ref.at[:, wide] for ref in raws],
+            halo_ref.at[:, :, wide],
+            conv_ref.at[:, :, wide],
+            decay_ref,
+            beta_ref,
+            rate_ref,
+            reset_ref,
+            d_out_ref.at[:, wide],
+            gain_ref.at[:, wide],
+            mixed_ref.at[:, wide],
+            stat_ref,
+            y_ref.at[:, :, wide],
+            *[ref.at[some] for ref in (*kept, state_ref, grad_ref)],
+            *[ref.at[:, wide] for ref in (out_ref, dq_ref, dk_ref, dv_ref, edge_ref, back_ref, param_ref)],
+            d_decay_ref,
+            d_beta_ref,
+            padded,
+            d_conv,
+        )
+        return carry
+
+    lax.fori_loop(0, steps, backward, 0)
+
+    for step in range(1, partners):
+        stat_copy(lax.rem(mine + step, partners), mine).wait_send()
+
+    @pl.when(place < count - 1)
+    def _():
+        def done(h, carry):
+            state_copy(h).wait_send()
+            return carry
+
+        lax.fori_loop(0, heads, done, 0)
+
+    @pl.when(place > 0)
+    def _():
+        def done(h, carry):
+            grad_copy(h).wait_send()
+            return carry
+
+        lax.fori_loop(0, heads, done, 0)
 
     back = pltpu.make_async_remote_copy(
         src_ref=back_ref,
@@ -603,7 +676,7 @@
 
     def near(target, slot):
         return pltpu.make_async_remote_copy(
-            src_ref=param_ref.at[target],
+            src_ref=param_ref.at[pl.ds(pl.multiple_of(target * rows, rows), rows)],
             dst_ref=near_land.at[slot],
             send_sem=near_send.at[target],
             recv_sem=near_recv.at[slot],
@@ -623,7 +696,7 @@
 
     def final(target, slot):
         return pltpu.make_async_remote_copy(
-            src_ref=final_land.at[mine],
+            src_ref=final_land.at[core],
             dst_ref=final_land.at[slot],
             send_sem=final_send.at[target],
             recv_sem=final_recv.at[slot],
@@ -642,8 +715,8 @@
         for step in range(1, total):
             copy(lax.rem(here + step, total), here).wait_send()
 
-    near_land[mine] = param_ref[mine]
-    exchange(near, mine, pairs)
+    near_land[core] = param_ref[pl.ds(pl.multiple_of(core * rows, rows), rows), :]
+    exchange(near, core, pairs)
     part = near_land[0]
     for slot in range(1, pairs):
         part = part + near_land[slot]
@@ -652,8 +725,8 @@
     part = far_land[0]
     for slot in range(1, count):
         part = part + far_land[slot]
-    final_land[mine] = part
-    exchange(final, mine, pairs)
+    final_land[core] = part
+    exchange(final, core, pairs)
     total_ref[...] = final_land[...]
 
     @pl.when(place == count - 1)
@@ -665,9 +738,9 @@
         back.wait_recv()
         arrived_ref[...] = back_land[...]
 
-    settle(near, mine, pairs)
+    settle(near, core, pairs)
     settle(far, place, count)
-    settle(final, mine, pairs)
+    settle(final, core, pairs)
 
     @pl.when(place > 0)
     def _():
@@ -675,8 +748,12 @@
 
 
 def final_kernel(
-    q_ref, k_ref, v_ref, edge_ref, come_ref, total_ref, dq_ref, dk_ref, dv_ref, conv_ref, gain_ref, rate_ref
+    o_ref, decay_ref, beta_ref, q_ref, k_ref, v_ref, edge_ref, come_ref, total_ref,
+    out_ref, d_decay_ref, d_beta_ref, dq_ref, dk_ref, dv_ref, conv_ref, gain_ref, rate_ref,
 ):
+    out_ref[...] = o_ref[...]
+    d_decay_ref[...] = decay_ref[...]
+    d_beta_ref[...] = beta_ref[...]
     length, width = q_ref.shape
     numbers, taps = conv_ref.shape[:2]
     heads = rate_ref.shape[1]
@@ -726,7 +803,6 @@
     partners = lax.axis_size("head")
     pairs = lax.axis_size("dp")
     group = 4 if heads % 4 == 0 else 1
-    steps = heads // group
     span = group * size
     vmem = pl.BlockSpec(memory_space=pltpu.VMEM)
     shape = jax.ShapeDtypeStruct
@@ -736,120 +812,64 @@
     rate = decay_rate[None, :]
     decay, beta = decay_logit[0].T, beta_logit[0].T
 
-    halo = pl.pallas_call(
-        functools.partial(halo_kernel, count),
-        out_shape=shape((3, TILE, width), BF16),
-        in_specs=[pl.BlockSpec(memory_space=pl.ANY)] * 3,
-        out_specs=vmem,
-        scratch_shapes=[pltpu.VMEM((3, TILE, width), BF16), dma((3,)), dma((3,))],
-        compiler_params=remote_params(0),
-        name="halo",
-    )(*raws)
-
-    cols = pl.BlockSpec((tokens, span), lambda i: (0, i))
-    halo_cols = pl.BlockSpec((3, TILE, span), lambda i: (0, 0, i))
-    conv_cols = pl.BlockSpec((3, taps, span), lambda i: (0, 0, i))
-    y_cols = pl.BlockSpec((3, tokens, span), lambda i: (0, 0, i))
-    gate_all = pl.BlockSpec((heads, tokens), lambda i: (0, 0))
-    rate_all = pl.BlockSpec((1, heads), lambda i: (0, 0))
     flag = pl.BlockSpec(memory_space=pltpu.SMEM)
-    square = pl.BlockSpec((group, tokens, size), lambda i: (i, 0, 0))
-    matrix = shape((heads, tokens, size), F32)
-    local = pl.pallas_call(
-        functools.partial(local_kernel, group),
-        grid=(steps,),
-        out_shape=[shape((3, tokens, width), F32)] + [matrix] * 10,
-        in_specs=[cols] * 3 + [halo_cols, conv_cols, gate_all, gate_all, rate_all, flag],
-        out_specs=[y_cols] + [square] * 10,
-        scratch_shapes=[pltpu.VMEM((tokens + 8, span), F32)],
-        compiler_params=pltpu.CompilerParams(vmem_limit_bytes=VMEM_BYTES),
-        name="local",
-    )(*raws, halo, conv_weight, decay, beta, rate, block_resets)
-    y, query, key, inverse, attn, reach_key, base, reach, mix, carry_p, carry_q = local
-
-    buffer = pltpu.VMEM((heads, size, size), F32)
-    mixed, stat, state, grad = pl.pallas_call(
-        functools.partial(chain_kernel, count, partners),
-        out_shape=[
-            shape((tokens, width), F32),
-            shape((tokens, size), F32),
-            shape((heads, size, size), F32),
-            shape((heads, size, size), F32),
-        ],
-        in_specs=[vmem] * 6,
-        out_specs=[vmem] * 4,
-        scratch_shapes=[buffer] * 4
-        + [pltpu.VMEM((partners, tokens, size), F32)]
-        + [dma((heads,))] * 4
-        + [dma((partners,))] * 2,
-        compiler_params=remote_params(1),
-        name="chain",
-    )(mix, reach, carry_p, carry_q, d_out[0], gain)
-
-    gain_cols = pl.BlockSpec((1, span), lambda i: (0, i))
-    stat_all = pl.BlockSpec((tokens, size), lambda i: (0, 0))
-    rows = lambda n: pl.BlockSpec((n, span), lambda i: (0, i))
     wide = shape((tokens, width), BF16)
-    out, d_q, d_k, d_v, edge, back, param, d_decay, d_beta = pl.pallas_call(
-        functools.partial(back_kernel, group, width * partners),
-        grid=(steps,),
+    gate = shape((heads, tokens), F32)
+    lines = 16
+    part = lines // pairs
+    buffer = pltpu.VMEM((heads, tokens, size), F32)
+    square = pltpu.VMEM((heads, size, size), F32)
+    out, d_q, d_k, d_v, edge, d_decay, d_beta, total, arrived = pl.pallas_call(
+        functools.partial(mixer_kernel, count, partners, pairs, group),
         out_shape=[wide] * 4
         + [
             shape((24, width), F32),
+            gate,
+            gate,
+            shape((pairs, part, width), F32),
             shape((32, width), BF16),
-            shape((16, width), F32),
-            shape((heads, tokens), F32),
-            shape((heads, tokens), F32),
         ],
-        in_specs=[cols] * 3
-        + [halo_cols, conv_cols, gate_all, gate_all, rate_all, flag]
-        + [cols, gain_cols, cols, stat_all, y_cols]
-        + [square] * 8,
-        out_specs=[cols] * 4 + [rows(24), rows(32), rows(16), gate_all, gate_all],
-        scratch_shapes=[
+        in_specs=[vmem] * 7 + [flag] + [vmem] * 2,
+        out_specs=[vmem] * 9,
+        scratch_shapes=[pltpu.VMEM((3, tokens, width), F32)]
+        + [buffer] * 8
+        + [square] * 8
+        + [
+            pltpu.VMEM((tokens, width), F32),
+            pltpu.VMEM((tokens, size), F32),
+            pltpu.VMEM((partners, tokens, size), F32),
+            pltpu.VMEM((3, TILE, width), BF16),
+            pltpu.VMEM((3, TILE, width), BF16),
+            pltpu.VMEM((32, width), BF16),
+            pltpu.VMEM((32, width), BF16),
+            pltpu.VMEM((lines, width), F32),
+            pltpu.VMEM((pairs, part, width), F32),
+            pltpu.VMEM((count, part, width), F32),
+            pltpu.VMEM((pairs, part, width), F32),
             pltpu.VMEM((tokens + 8, span), F32),
             pltpu.VMEM((tokens + 16, span), F32),
-        ],
-        compiler_params=pltpu.CompilerParams(vmem_limit_bytes=VMEM_BYTES),
-        name="back",
-    )(
-        *raws, halo, conv_weight, decay, beta, rate, block_resets, d_out[0], gain, mixed, stat,
-        y, query, key, inverse, attn, reach_key, base, state, grad,
-    )
-
-    rows_each = 16 // pairs
-    total, arrived = pl.pallas_call(
-        functools.partial(sum_kernel, count, pairs),
-        out_shape=[shape((pairs, rows_each, width), F32), shape((32, width), BF16)],
-        in_specs=[vmem] * 2,
-        out_specs=[vmem] * 2,
-        scratch_shapes=[
-            pltpu.VMEM((pairs, rows_each, width), F32),
-            pltpu.VMEM((count, rows_each, width), F32),
-            pltpu.VMEM((pairs, rows_each, width), F32),
-            pltpu.VMEM((32, width), BF16),
-            dma((pairs,)),
-            dma((pairs,)),
-            dma((count,)),
-            dma((count,)),
-            dma((pairs,)),
-            dma((pairs,)),
-            dma,
-            dma,
-        ],
-        compiler_params=remote_params(2),
-        name="sums",
-    )(param.reshape(pairs, rows_each, width), back)
+        ]
+        + [dma((3,))] * 2
+        + [dma((heads,))] * 4
+        + [dma((partners,))] * 2
+        + [dma((pairs,))] * 2
+        + [dma((count,))] * 2
+        + [dma((pairs,))] * 2
+        + [dma] * 2,
+        compiler_params=remote_params(0),
+        name="mixer",
+    )(*raws, conv_weight, decay, beta, rate, block_resets, d_out[0], gain)
     total = total.reshape(16, width)
-    d_q, d_k, d_v, d_conv, d_gain, d_rate = pl.pallas_call(
+    out, d_decay, d_beta, d_q, d_k, d_v, d_conv, d_gain, d_rate = pl.pallas_call(
         final_kernel,
-        out_shape=[wide] * 3
+        out_shape=[wide, gate, gate]
+        + [wide] * 3
         + [shape((3, taps, width), F32), shape((1, width), F32), shape((1, heads), F32)],
-        in_specs=[vmem] * 6,
-        out_specs=[vmem] * 6,
+        in_specs=[vmem] * 9,
+        out_specs=[vmem] * 9,
         compiler_params=pltpu.CompilerParams(vmem_limit_bytes=VMEM_BYTES),
         name="final",
-    )(d_q, d_k, d_v, edge, arrived, total)
+    )(out, d_decay, d_beta, d_q, d_k, d_v, edge, arrived, total)
     return (
         out[None],
         d_q[None],

time: 94.3 us -> 75.4 us (0.80)
  Pallas kernels: 92.7 us -> 73.9 us
    pallas_call x6 -> x2, Pallas kernels: 92.7 us -> 73.9 us  [the longest x1 71.7 us: body(): pl.pallas_call(functools.partial(mixer_kernel, count, partners, pairs, gr...]
where the time goes in v3:
time: 75.4 us; the launch traced here: 75.2 us
  Pallas kernels  73.9 us (98%)
  between operations  1.3 us (2%)
    pallas_call x1, Pallas kernels, body(): pl.pallas_call(functools.partial(mixer_kernel, count, partners, pairs, gr...  71.7 us
    pallas_call x1, Pallas kernels, body(): pl.pallas_call(final_kernel, out_shape=[wide, gate, gate] + [wide] * 3 +...  2.25 us

profile of v3, /device:TPU:0, one launch (start us, length us, event | category | flops | bytes accessed | tf_op | source)
XLA Modules:
  0.0 75.2 jit_solution(10881470075024802450)
XLA Ops:
  1.3 71.7 %mixer.1 = (bf16[128,1024]{1,0:T(8,128)(2,1)}, bf16[128,1024]{1,0:T(8,128)(2,1)}, bf16[128,1024]{1,0:T(8,128)(2,1)}, bf16[128,1024]{1,0:T(8,128)(2,1)}, f32[24,1...) custom-call(bf16[128,1024]{1,0:T(8,128)(2,1)} %bitcast.25, ...), custom_call_target="tpu_custom_call" | custom-call | tf_op jit(solution)/shard_map/mixer/pallas_call | solution.py:822
  73.0 2.2 %final.1 = (bf16[128,1024]{1,0:T(8,128)(2,1)}, f32[8,128]{1,0:T(8,128)}, f32[8,128]{1,0:T(8,128)}, bf16[128,1024]{1,0:T(8,128)(2,1)}, bf16[128,1024]{1,0:T(8,128...) custom-call(bf16[128,1024]{1,0:T(8,128)(2,1)} %get-tuple-element.27.o_ref, ...), custom_call_target="tpu_custom_call" | custom-call | tf_op jit(solution)/shard_map/final/pallas_call | solution.py:863

commit v4 on v3

--- a/solution.py
+++ b/solution.py
@@ -463,11 +463,6 @@
             halo_copy(number).wait_recv()
         halo_ref[...] = halo_land[...]
 
-    @pl.when(place < count - 1)
-    def _():
-        for number in range(3):
-            halo_copy(number).wait_send()
-
     def state_copy(h):
         return pltpu.make_async_remote_copy(
             src_ref=state_out.at[h],
@@ -519,24 +514,23 @@
 
     lax.fori_loop(0, steps, forward, 0)
 
-    @pl.when(place > 0)
-    def _():
-        def hop(h, carry):
-            state_copy(h).wait_recv()
-            entering = state_land[h]
-            state_ref[h] = entering
-
-            @pl.when(place < count - 1)
-            def _():
-                state_out[h] = carry_q_ref[h] + dot3(pair(entering), pair(carry_p_ref[h]), NN)
-                state_copy(h).start()
-
-            return carry
-
-        lax.fori_loop(0, heads, hop, 0)
+    def enter(h):
+        state_copy(h).wait_recv()
+        entering = state_land[h]
+        state_ref[h] = entering
+
+        @pl.when(place < count - 1)
+        def _():
+            state_out[h] = carry_q_ref[h] + dot3(pair(entering), pair(carry_p_ref[h]), NN)
+            state_copy(h).start()
 
     def mixing(h, carry):
         square, inner = carry
+
+        @pl.when(place > 0)
+        def _():
+            enter(h)
+
         cols = pl.ds(pl.multiple_of(h * size, size), size)
         mixed = mix_ref[h] + dot3(pair(reach_ref[h]), pair(state_ref[h]), NT)
         mixed_ref[:, cols] = mixed
@@ -737,6 +731,11 @@
     def _():
         back.wait_recv()
         arrived_ref[...] = back_land[...]
+
+    @pl.when(place < count - 1)
+    def _():
+        for number in range(3):
+            halo_copy(number).wait_send()
 
     settle(near, core, pairs)
     settle(far, place, count)

time: 75.4 us -> 73.9 us (0.980)
  Pallas kernels: 73.9 us -> 72.5 us
    pallas_call x1, Pallas kernels: 71.7 us -> 70.2 us  [body(): pl.pallas_call(functools.partial(mixer_kernel, count, partners, pairs, gr...]
where the time goes in v4:
time: 73.9 us; the launch traced here: 73.8 us
  Pallas kernels  72.5 us (98%)
  between operations  1.3 us (2%)
    pallas_call x1, Pallas kernels, body(): pl.pallas_call(functools.partial(mixer_kernel, count, partners, pairs, gr...  70.2 us
    pallas_call x1, Pallas kernels, body(): pl.pallas_call(final_kernel, out_shape=[wide, gate, gate] + [wide] * 3 +...  2.25 us

profile of v4, /device:TPU:0, one launch (start us, length us, event | category | flops | bytes accessed | tf_op | source)
XLA Modules:
  0.0 73.8 jit_solution(160685458892986257)
XLA Ops:
  1.3 70.2 %mixer.1 = (bf16[128,1024]{1,0:T(8,128)(2,1)}, bf16[128,1024]{1,0:T(8,128)(2,1)}, bf16[128,1024]{1,0:T(8,128)(2,1)}, bf16[128,1024]{1,0:T(8,128)(2,1)}, f32[24,1...) custom-call(bf16[128,1024]{1,0:T(8,128)(2,1)} %bitcast.25, ...), custom_call_target="tpu_custom_call" | custom-call | tf_op jit(solution)/shard_map/mixer/pallas_call | solution.py:821
  71.5 2.2 %final.1 = (bf16[128,1024]{1,0:T(8,128)(2,1)}, f32[8,128]{1,0:T(8,128)}, f32[8,128]{1,0:T(8,128)}, bf16[128,1024]{1,0:T(8,128)(2,1)}, bf16[128,1024]{1,0:T(8,128...) custom-call(bf16[128,1024]{1,0:T(8,128)(2,1)} %get-tuple-element.27.o_ref, ...), custom_call_target="tpu_custom_call" | custom-call | tf_op jit(solution)/shard_map/final/pallas_call | solution.py:862
